TPU v7x, 1024 devices: a whole 4x4x32 slice. The times are simulated.
1024 devices in a mesh: seq: 64 (over z, core), head: 16 (over x, y).
Axes of the slice: x: 4, y: 4, z: 32, core: 2. Of those that a mesh axis runs over, the one named last changes fastest.
Arguments:
- queries_first: bfloat16 [8192, 8192], P('seq', 'head'), may hold values from -6 to 6
- keys_first: bfloat16 [8192, 8192], P('seq', 'head'), may hold values from -6 to 6
- values_first: bfloat16 [8192, 8192], P('seq', 'head'), may hold values from -6 to 6
- queries_second: bfloat16 [8192, 8192], P('seq', 'head'), may hold values from -6 to 6
- rates: float32 [16, 8192], P('head', 'seq'), may hold values from 0.05 to 1
- gate_memory: bfloat16 [16, 512, 512], P('head'), may hold values from -0.25 to 0.25
- up_memory: bfloat16 [16, 512, 512], P('head'), may hold values from -0.25 to 0.25
- down_memory: bfloat16 [16, 512, 512], P('head'), may hold values from -0.25 to 0.25
- out_proj: bfloat16 [8192, 512], P('head'), may hold values from -0.0625 to 0.0625
Outputs:
- projected: bfloat16 [8192, 1024], P(('seq', 'head'))
All inputs are finite; a program needn't handle non-finite values.
Results may differ from a plain program's by a relative error of at most 0.018.
Values may be sent and summed in bfloat16 or wider, within the bound.
No kernel may reach another device: no remote copies, remote signals or barrier semaphores. Data moves between devices by JAX's collectives and lax.ppermute only.
A program may use at most 32 MiB of HBM per device.

v0:
```python
import jax
import jax.numpy as jnp
from jax import lax
from jax.sharding import PartitionSpec as P

NS_ITERS = 2


first_coeff = 3.4445
second_coeff = -4.775
third_coeff = 2.0315
step_scale = 0.5


def apply_memory(inputs, w_gate, w_up, w_down):
    gating = jnp.dot(inputs, w_gate, preferred_element_type=jnp.float32)
    lifted = jnp.dot(inputs, w_up, preferred_element_type=jnp.float32)
    hidden = (jax.nn.silu(gating) * lifted).astype(jnp.bfloat16)
    return jnp.dot(hidden, w_down, preferred_element_type=jnp.float32).astype(jnp.bfloat16)


def orthogonalize(matrix):
    widened = matrix.astype(jnp.float32)
    magnitude = jnp.sqrt(jnp.sum(widened * widened)) + 1e-07
    current = (widened / magnitude).astype(jnp.bfloat16)
    for step in range(NS_ITERS):
        gram_matrix = lax.optimization_barrier(
            jnp.dot(current, current.T, preferred_element_type=jnp.float32).astype(jnp.bfloat16)
        )
        square = jnp.dot(gram_matrix, gram_matrix, preferred_element_type=jnp.float32)
        polynomial = (second_coeff * gram_matrix.astype(jnp.float32) + third_coeff * square).astype(
            jnp.bfloat16
        )
        mixed = jnp.dot(polynomial, current, preferred_element_type=jnp.float32)
        current = (first_coeff * current.astype(jnp.float32) + mixed).astype(jnp.bfloat16)
    return current


def updated(memory, direction):
    return (memory.astype(jnp.float32) + step_scale * direction.astype(jnp.float32)).astype(
        jnp.bfloat16
    )


def on_device(
    queries_first,
    keys_first,
    values_first,
    queries_second,
    rates,
    gate_memory,
    up_memory,
    down_memory,
    out_proj,
):
    w_gate = gate_memory[0]
    w_up = up_memory[0]
    w_down = down_memory[0]
    width = keys_first.shape[1]
    hidden_width = w_gate.shape[1]
    first_out = apply_memory(queries_first, w_gate, w_up, w_down)
    gating = jnp.dot(keys_first, w_gate, preferred_element_type=jnp.float32)
    lifted = jnp.dot(keys_first, w_up, preferred_element_type=jnp.float32)
    sigmoid_gate = jax.nn.sigmoid(gating)
    activated = gating * sigmoid_gate
    hidden = (activated * lifted).astype(jnp.bfloat16)
    scaled = (rates[0][:, None] * values_first.astype(jnp.float32)).astype(jnp.bfloat16)
    backward = jnp.dot(scaled, w_down.T, preferred_element_type=jnp.float32)
    gate_back = (backward * lifted * sigmoid_gate * (1.0 + gating * (1.0 - sigmoid_gate))).astype(
        jnp.bfloat16
    )
    up_back = (backward * activated).astype(jnp.bfloat16)
    stacked = jnp.concatenate(
        [
            jnp.dot(keys_first.T, gate_back, preferred_element_type=jnp.float32),
            jnp.dot(keys_first.T, up_back, preferred_element_type=jnp.float32),
            jnp.dot(scaled.T, hidden, preferred_element_type=jnp.float32),
        ],
        axis=0,
    )
    summed_rows = lax.psum_scatter(stacked, "seq", scatter_dimension=0, tiled=True).astype(
        jnp.bfloat16
    )
    gathered = lax.all_gather(summed_rows, "seq", axis=0, tiled=True).reshape(
        3, width, hidden_width
    )
    results = [orthogonalize(gathered[member]) for member in range(3)]
    new_gate = updated(w_gate, results[0])
    new_up = updated(w_up, results[1])
    new_down = updated(w_down, results[2].T)
    second_out = apply_memory(queries_second, new_gate, new_up, new_down)
    return lax.psum_scatter(
        jnp.concatenate(
            [
                jnp.dot(first_out, out_proj, preferred_element_type=jnp.float32),
                jnp.dot(second_out, out_proj, preferred_element_type=jnp.float32),
            ],
            axis=1,
        ).astype(jnp.bfloat16),
        "head",
        scatter_dimension=0,
        tiled=True,
    )


def solution(mesh):
    in_specs = (
        P("seq", "head"),
        P("seq", "head"),
        P("seq", "head"),
        P("seq", "head"),
        P("head", "seq"),
        P("head", None, None),
        P("head", None, None),
        P("head", None, None),
        P("head", None),
    )
    out_specs = P(("seq", "head"), None)
    return jax.shard_map(
        on_device, mesh=mesh, in_specs=in_specs, out_specs=out_specs, check_vma=False
    )
```

profile of v0, /device:TPU:1, one launch (start us, length us, event | category | flops | bytes accessed | tf_op | source)
XLA Modules:
  0.0 552.3 jit_solution(5144788268982703368)
XLA Ops:
  6.6 1.4 fusion.70
  8.0 1.3 fusion.67
  9.4 0.3 fusion.61
  9.7 0.4 convolution_bitcast_fusion
  10.1 0.4 convolution_bitcast_fusion.1
  10.5 0.4 fusion.88
  10.9 2.0 pad_maximum_fusion
  12.9 219.0 %reduce-scatter.2.cloned.1.call-done = f32[24,512]{1,0:T(8,128)} async-done(((f32[1536,512]{1,0:T(8,128)}), f32[24,512]{1,0:T(8,128)}) %reduce-scatter.2.cloned.1.call-update) | async-done | bytes 49168 | tf_op jit(solution)/shard_map/reduce_scatter | solution.py:81
  231.9 1.4 convert_element_type.187
  233.4 1.0 copy.12
  234.9 0.4 convolution_convert_fusion.7
  235.3 135.6 %all-gather.2.cloned.1.call-done = bf16[1536,512]{1,0:T(8,128)(2,1)} async-done(((bf16[24,512]{1,0:T(8,128)(2,1)}), bf16[1536,512]{1,0:T(8,128)(2,1)}) %all-gather.2.cloned.1.call-update) | async-done | bytes 1572880 | tf_op jit(solution)/shard_map/all_gather | solution.py:84
  370.9 2.5 fusion.44
  374.1 1.3 convolution_convert_fusion.1
  375.4 2.2 fusion.24
  377.5 0.5 convolution_convert_fusion
  378.0 1.2 fusion.11
  380.0 1.3 convolution_convert_fusion.5
  381.3 2.5 fusion.12
  383.8 0.5 convolution_convert_fusion.4
  384.2 1.2 fusion.7
  386.1 1.7 convolution_convert_fusion.3
  387.8 2.0 fusion.18
  389.8 0.5 convolution_convert_fusion.2
  390.3 1.2 fusion.9
  391.5 2.5 fusion.34
  394.0 1.8 fusion.38
  395.8 1.7 fusion.39
  397.8 0.7 pad_maximum_fusion.1
  398.6 1.3 dynamic-slice
  400.5 143.9 %all-reduce.3.cloned.1.call-done = bf16[128,1024]{1,0:T(8,128)(2,1)} async-done(((bf16[128,1024]{1,0:T(8,128)(2,1)}), bf16[128,1024]{1,0:T(8,128)(2,1)}) %all-reduce.3.cloned.1.call-update) | async-done | bytes 262160
  544.4 1.3 constant_dynamic-slice_fusion
  (33 shorter events, 0.9 us)
Async XLA Ops:
  6.5 228.3 %copy-start = (bf16[512,512]{1,0:T(8,128)(2,1)S(1)}, bf16[512,512]{1,0:T(8,128)(2,1)}, u32[]{:S(2)}) copy-start(bf16[512,512]{1,0:T(8,128)(2,1)} %param.17) | copy-start | bytes 1572868
  6.5 3.2 copy-start.3
  6.5 2.8 copy-start.10
  6.5 2.8 copy-start.5
  6.5 2.9 copy-start.1
  6.5 225.3 %reduce-scatter.2.cloned.1.call-start = ((), (), s32[]{:S(2)}) async-start(), calls=%async_computation.1 | async-start | bytes 3194880 | tf_op jit(solution)/shard_map/reduce_scatter | solution.py:81
  12.8 221.5 %copy-start.2 = (bf16[1,512,512]{2,1,0:T(8,128)(2,1)S(1)}, bf16[1,512,512]{2,1,0:T(8,128)(2,1)}, u32[]{:S(2)}) copy-start(bf16[1,512,512]{2,1,0:T(8,128)(2,1)} %param.14) | copy-start | bytes 1572868
  12.8 221.5 %copy-start.9 = (bf16[128,512]{1,0:T(8,128)(2,1)S(1)}, bf16[128,512]{1,0:T(8,128)(2,1)}, u32[]{:S(2)}) copy-start(bf16[128,512]{1,0:T(8,128)(2,1)} %param.9) | copy-start | bytes 393220
  12.9 221.7 %copy-start.6 = (bf16[1,512,512]{2,1,0:T(8,128)(2,1)S(1)}, bf16[1,512,512]{2,1,0:T(8,128)(2,1)}, u32[]{:S(2)}) copy-start(bf16[1,512,512]{2,1,0:T(8,128)(2,1)} %param.15) | copy-start | bytes 1572868
  12.9 358.0 %all-gather.2.cloned.1.call-start = ((), (), s32[]{:S(2)}) async-start(), calls=%async_computation.2 | async-start | bytes 1597440 | tf_op jit(solution)/shard_map/all_gather | solution.py:84
  233.3 311.1 %all-reduce.3.cloned.1.call-start = ((), (), s32[]{:S(2)}) async-start(), calls=%async_computation.3 | async-start | bytes 524288
  370.9 3.2 copy-start.4
  389.8 1.7 copy-start.11
  391.5 2.5 copy-start.7
  394.0 1.8 copy-start.8
Sparse Core Ops, SparseCore 0:
  13.0 218.8 reduce-scatter.1
  234.9 135.9 all-gather.1
  398.7 145.6 all-reduce.2
where the time goes:
time: 553 us; the launch traced here: 552 us
  waiting for transfers between devices  499 us (90%)
  matrix products  27.4 us (5%)
  between operations  16 us (3%)
  other arithmetic  6.54 us (1%)
    reduce_scatter x1, waiting for transfers between devices, on_device(): lax.psum_scatter(stacked, 'seq', scatter_dimension=0, tiled=True)  219 us
    unnamed x4, waiting for transfers between devices  144 us
    all_gather x1, waiting for transfers between devices, on_device(): lax.all_gather(summed_rows, 'seq', axis=0, tiled=True)  136 us
  transfers between devices with their start and end apart: 3, of which 3 were waited for; matrix products, arithmetic and copies ran while one was open for 1% of the time, Pallas kernels for 0%

commit v1 on v0

v1 whole, which is shorter than its diff:
```python
import jax
import jax.numpy as jnp
from jax import lax
from jax.sharding import Mesh
from jax.sharding import PartitionSpec as P

NS_ITERS = 2
FAR, NEAR, CORES, SIDE = 8, 4, 2, 4
ROWS = 8

first_coeff = 3.4445
second_coeff = -4.775
third_coeff = 2.0315
step_scale = 0.5

f32 = jnp.float32
bf16 = jnp.bfloat16
SWAP = [(0, 1), (1, 0)]


def dot(a, b, contract):
    return lax.dot_general(a, b, ((contract[:1], contract[1:]), ((), ())), preferred_element_type=f32)


def apply_memory(inputs, w_gate, w_up, w_down, side):
    gating = dot(inputs, w_gate, (1, side))
    lifted = dot(inputs, w_up, (1, side))
    hidden = (jax.nn.silu(gating) * lifted).astype(bf16)
    return dot(hidden, w_down, (1, 0)).astype(bf16)


def orthogonalize_transposed(matrix):
    widened = matrix.astype(f32)
    magnitude = jnp.sqrt(jnp.sum(widened * widened)) + 1e-07
    current = (widened / magnitude).astype(bf16)
    for step in range(NS_ITERS):
        gram = dot(current, current, (0, 0)).astype(bf16)
        square = dot(gram, gram, (1, 0))
        polynomial = (second_coeff * gram.astype(f32) + third_coeff * square).astype(bf16)
        mixed = dot(current, polynomial, (1, 0))
        current = (first_coeff * current.astype(f32) + mixed).astype(bf16)
    return current


def updated(memory, direction):
    return (memory.astype(f32) + step_scale * direction.astype(f32)).astype(bf16)


def head_sum(share):
    pieces = lax.all_to_all(share, ("x", "y"), 0, 0, tiled=True)
    pieces = pieces.reshape(SIDE * SIDE, -1, share.shape[1])
    return jnp.sum(pieces.astype(f32), axis=0)


def on_device(q_first, keys, values, q_second, rates, gate_memory, up_memory, down_memory, out_proj):
    core = lax.axis_index("core")
    near = lax.axis_index("near")
    w_gate, w_up, w_down = gate_memory[0], up_memory[0], down_memory[0]
    tokens, width = keys.shape
    gate_t, up_t = w_gate.T, w_up.T

    scaled = (rates[0][:, None] * values.astype(f32)).astype(bf16)
    all_keys = lax.all_gather(keys, "near", axis=0, tiled=True)
    all_scaled = lax.all_gather(scaled, "near", axis=0, tiled=True)

    def share(w):
        rows = w.reshape(CORES, NEAR, FAR * ROWS, width)
        return lax.dynamic_index_in_dim(rows, near, 1, keepdims=False).reshape(-1, width)

    gating = dot(share(gate_t), all_keys, (1, 1))
    lifted = dot(share(up_t), all_keys, (1, 1))
    s = jax.nn.sigmoid(gating)
    activated = gating * s
    hidden = (activated * lifted).astype(bf16)
    backward = dot(share(w_down), all_scaled, (1, 1))
    gate_back = (backward * lifted * s * (1.0 + gating * (1.0 - s))).astype(bf16)
    up_back = (backward * activated).astype(bf16)
    partial = jnp.stack(
        [
            dot(gate_back, all_keys, (1, 0)),
            dot(up_back, all_keys, (1, 0)),
            dot(hidden, all_scaled, (1, 0)),
        ]
    ).reshape(3, CORES, FAR, ROWS, width)
    kept = jnp.where(core == 0, partial[:, 0], partial[:, 1])
    given = jnp.where(core == 0, partial[:, 1], partial[:, 0]).astype(bf16)
    taken = lax.ppermute(given, "core", SWAP)
    pieces = (kept + taken.astype(f32)).astype(bf16).transpose(1, 0, 2, 3)
    pieces = lax.all_to_all(pieces, "far", 0, 0, tiled=True)
    summed = jnp.sum(pieces.astype(f32), axis=0).astype(bf16)
    own = lax.all_gather(summed, "far", axis=0, tiled=False)
    own = lax.all_gather(own, "near", axis=0, tiled=False)
    other = lax.ppermute(own, "core", SWAP)
    halves = jnp.stack([jnp.where(core == 0, own, other), jnp.where(core == 0, other, own)])
    matrices = halves.transpose(3, 0, 1, 2, 4, 5).reshape(3, -1, width)

    results = [orthogonalize_transposed(matrices[m]) for m in range(3)]
    new_gate = updated(gate_t, results[0])
    new_up = updated(up_t, results[1])
    new_down = updated(w_down, results[2])
    first_out = apply_memory(q_first, w_gate, w_up, w_down, 0)
    second_out = apply_memory(q_second, new_gate, new_up, new_down, 1)
    both = jnp.concatenate(
        [dot(first_out, out_proj, (1, 0)), dot(second_out, out_proj, (1, 0))], axis=1
    ).astype(bf16)
    return head_sum(both).astype(bf16)


def solution(mesh):
    fine = Mesh(
        mesh.devices.reshape(FAR, NEAR, CORES, SIDE, SIDE), ("far", "near", "core", "x", "y")
    )
    seq, head = ("far", "near", "core"), ("x", "y")
    in_specs = (
        P(seq, head),
        P(seq, head),
        P(seq, head),
        P(seq, head),
        P(head, seq),
        P(head, None, None),
        P(head, None, None),
        P(head, None, None),
        P(head, None),
    )
    out_specs = P(seq + head, None)
    return jax.shard_map(
        on_device, mesh=fine, in_specs=in_specs, out_specs=out_specs, check_vma=False
    )
```

time: 553 us -> 203 us (0.37)
  waiting for transfers between devices: 499 us -> 1.05 us
  blocking collectives: 0 us -> 134 us
  starting transfers between devices: 0.12 us -> 30.9 us
  between operations: 16 us -> 2.35 us
    reduce_scatter x1 -> x0, waiting for transfers between devices: 219 us -> none  [on_device(): lax.psum_scatter(stacked, 'seq', scatter_dimension=0, tiled=True)]
    unnamed x4 -> x0, waiting for transfers between devices: 144 us -> none
    all_gather x1 -> x0, waiting for transfers between devices: 136 us -> none  [on_device(): lax.all_gather(summed_rows, 'seq', axis=0, tiled=True)]
    all_gather x0 -> x4, blocking collectives: none -> 77 us  [the longest x1 34.6 us: on_device(): own = lax.all_gather(summed, 'far', axis=0, tiled=False)]
    all_to_all x0 -> x2, blocking collectives: none -> 56.5 us  [the longest x1 42.4 us: on_device(): pieces = lax.all_to_all(pieces, 'far', 0, 0, tiled=True)]
    ppermute x0 -> x2, starting transfers between devices: none -> 30.9 us  [the longest x1 18.9 us: on_device(): taken = lax.ppermute(given, 'core', SWAP)]
  transfers between devices with their start and end apart: 3 -> 2, of which waited for: 3 -> 1; matrix products, arithmetic and copies ran while one was open for 1% -> 1% of each run, Pallas kernels for 0% -> 0%
where the time goes in v1:
time: 203 us
  blocking collectives  134 us (66%)
  starting transfers between devices  30.9 us (15%)
  matrix products  26.3 us (13%)
  other arithmetic  4.73 us (2%)
  local copies, waits for them, and re-layouts  3.92 us (2%)
  between operations  2.35 us (1%)
    all_to_all x1, blocking collectives, on_device(): pieces = lax.all_to_all(pieces, 'far', 0, 0, tiled=True)  42.4 us
    all_gather x1, blocking collectives, on_device(): own = lax.all_gather(summed, 'far', axis=0, tiled=False)  34.6 us
    dot_general x25, matrix products, dot(): lax.dot_general(a, b, ((contract[:1], contract[1:]), ((), ())), preferred...  26.3 us
    ppermute x1, starting transfers between devices, on_device(): taken = lax.ppermute(given, 'core', SWAP)  18.9 us
    all_gather x1, blocking collectives, on_device(): all_scaled = lax.all_gather(scaled, 'near', axis=0, tiled=True)  14.4 us
    all_gather x1, blocking collectives, on_device(): all_keys = lax.all_gather(keys, 'near', axis=0, tiled=True)  14.2 us
    all_to_all x1, blocking collectives, head_sum(): pieces = lax.all_to_all(share, ('x', 'y'), 0, 0, tiled=True)  14.1 us
    all_gather x1, blocking collectives, on_device(): own = lax.all_gather(own, 'near', axis=0, tiled=False)  13.8 us
  transfers between devices with their start and end apart: 2, of which 1 were waited for; matrix products, arithmetic and copies ran while one was open for 1% of the time, Pallas kernels for 0%

profile of v1, /device:TPU:1, one launch (start us, length us, event | category | flops | bytes accessed | tf_op | source)
XLA Modules:
  0.0 202.8 jit_solution(13433864909139187065)
XLA Ops:
  0.0 1.3 copy.27
  1.3 1.3 copy.28
  2.6 14.2 %all_gather.19 = bf16[512,512]{1,0:T(8,128)(2,1)S(1)} all-gather(bf16[128,512]{1,0:T(8,128)(2,1)S(1)} %copy-done.6), channel_id=1, replica_groups=mesh['far'=8,'near'=4,'core'=2,'x'=4,'y'=4] {'near'}, dimensions={0}, use_global_device_ids=true | all-gather | bytes 655360 | tf_op jit(solution)/shard_map/all_gather | solution.py:63
  17.5 0.9 constant_dynamic-slice_fusion.2
  18.5 14.4 %all_gather.18 = bf16[512,512]{1,0:T(8,128)(2,1)S(1)} all-gather(bf16[128,512]{1,0:T(8,128)(2,1)S(1)} %multiply_convert_fusion.3), channel_id=1, replica_groups=mesh['far'=8,'near'=4,'core'=2,'x'=4,'y'=4] {'near'}, dimensions={0}, use_global_device_ids=true | all-gather | bytes 655360 | tf_op jit(solution)/shard_map/all_gather | solution.py:64
  34.1 18.9 %collective-permute-start = (bf16[3,8,8,512]{3,2,0,1:T(8,128)(2,1)S(1)}, bf16[3,8,8,512]{3,2,0,1:T(8,128)(2,1)S(1)}, u32[]{:S(2)}, u32[]{:S(2)}) collective-permute-start(bf16[3,8,8,512]{3,2,0,1:T(8,128)(2,1)S(1)} %fusion.95), channel_id=1, source_target_pairs={{0,16},{16,0},{1,17},{17,1},{2,18},{18,2},{3,19},{19,3},{4,20},{20... | collective-permute-start | bytes 589832 | tf_op jit(solution)/shard_map/ppermute | solution.py:87
  53.0 1.0 collective-permute-done
  54.2 42.4 %all_to_all.11 = bf16[8,3,8,512]{3,2,1,0:T(8,128)(2,1)S(1)} all-to-all(bf16[8,3,8,512]{3,2,1,0:T(8,128)(2,1)S(1)} %fusion.96), channel_id=1, replica_groups=mesh['far'=8,'near'=4,'core'=2,'x'=4,'y'=4] {'far'}, dimensions={0} | all-to-all | bytes 393216 | tf_op jit(solution)/shard_map/all_to_all | solution.py:89
  96.6 34.6 %all-gather = bf16[24,8,512]{2,1,0:T(8,128)(2,1)S(1)} all-gather(bf16[3,8,512]{2,1,0:T(8,128)(2,1)S(1)} %reduce_sum.51), channel_id=2, replica_groups=mesh['far'=8,'near'=4,'core'=2,'x'=4,'y'=4] {'far'}, dimensions={0}, use_global_device_ids=true | all-gather | bytes 221184 | tf_op jit(solution)/shard_map/all_gather | solution.py:91
  131.2 13.8 %all-gather.1 = bf16[32,3,8,512]{3,2,1,0:T(8,128)(2,1)S(1)} all-gather(bf16[8,3,8,512]{3,2,1,0:T(8,128)(2,1)S(1)} %bitcast.157), channel_id=3, replica_groups=mesh['far'=8,'near'=4,'core'=2,'x'=4,'y'=4] {'near'}, dimensions={0}, use_global_device_ids=true | all-gather | bytes 983040 | tf_op jit(solution)/shard_map/all_gather | solution.py:92
  145.1 12.0 %collective-permute-start.1 = (bf16[4,8,3,8,512]{4,3,1,0,2:T(8,128)(2,1)S(1)}, bf16[4,8,3,8,512]{4,3,1,0,2:T(8,128)(2,1)}, u32[]{:S(2)}, u32[]{:S(2)}) collective-permute-start(bf16[4,8,3,8,512]{4,3,1,0,2:T(8,128)(2,1)S(1)} %bitcast.153), channel_id=1, source_target_pairs={{0,16},{16,0},{1,17},{17,1},{2,18},{18,2},{3,19},{19,3},{4,20},{20... | collective-permute-start | bytes 2359304 | tf_op jit(solution)/shard_map/ppermute | solution.py:93
  157.1 0.9 fusion.67
  158.1 1.5 convolution_convert_fusion.5
  159.8 1.2 select_bitcast_fusion.1
  161.2 1.1 fusion.48
  164.3 1.3 fusion.49
  165.6 0.5 fusion.12
  166.4 2.0 fusion.27
  168.4 0.5 convolution_convert_fusion
  168.9 1.2 fusion.14
  170.1 1.3 fusion.6
  171.4 2.2 %fusion.15 = bf16[512,512]{1,0:T(8,128)(2,1)S(1)} fusion(bf16[512,512]{1,0:T(8,128)(2,1)S(1)} %bitcast.159, bf16[512,512]{1,0:T(8,128)(2,1)} %fusion.6), kind=kOutput, calls=%fused_computation.40 | convolution fusion | flops 539230208 | bytes 1572864 | tf_op jit(solution)/shard_map/dot_general | solution.py:22
  174.1 1.2 fusion.8
  175.4 1.3 fusion.9
  176.6 3.0 %fusion.21 = bf16[512,512]{1,0:T(8,128)(2,1)} fusion(bf16[512,512]{1,0:T(8,128)(2,1)S(1)} %bitcast.158, bf16[512,512]{1,0:T(8,128)(2,1)} %fusion.9), kind=kOutput, calls=%fused_computation.46 | convolution fusion | flops 539230208 | bytes 1572864 | tf_op jit(solution)/shard_map/dot_general | solution.py:22
  179.7 1.7 convolution_convert_fusion.1
  181.4 1.2 fusion.11
  182.6 2.5 %fusion.36 = f32[128,512]{1,0:T(8,128)} fusion(bf16[128,512]{1,0:T(8,128)(2,1)S(1)} %copy-done.11, bf16[512,512]{1,0:T(8,128)(2,1)S(1)} %fusion.15, bf16[512,512]{1,0:T(8,128)(2,1)} %fusion.8, bf16[1,512,512]{1,2,0:T(8,128)(2,1)S(1)} %copy.27), kind=kOutput, calls=%fused_computation.61 | convolution fusion | flops 337903616 | bytes 1966080 | tf_op jit(solution)/shard_map/dot_general | solution.py:22
  185.1 1.9 fusion.40
  187.1 0.7 fusion.41
  188.0 14.1 %all_to_all.12 = bf16[16,8,1024]{2,1,0:T(8,128)(2,1)S(1)} all-to-all(bf16[16,8,1024]{2,1,0:T(8,128)(2,1)S(1)} %pad_maximum_fusion.1), channel_id=1, replica_groups=mesh['far'=8,'near'=4,'core'=2,'x'=4,'y'=4] {'x','y'}, dimensions={0} | all-to-all | bytes 524288 | tf_op jit(solution)/shard_map/all_to_all | solution.py:50
  202.1 0.6 reduce_sum.55
  (47 shorter events, 3.5 us)
Async XLA Ops:
  0.0 159.6 %copy-start = (bf16[512,512]{1,0:T(8,128)(2,1)S(1)}, bf16[512,512]{1,0:T(8,128)(2,1)}, u32[]{:S(2)}) copy-start(bf16[512,512]{1,0:T(8,128)(2,1)} %param.17) | copy-start | bytes 1572868
  0.0 2.6 %copy-start.6 = (bf16[128,512]{1,0:T(8,128)(2,1)S(1)}, bf16[128,512]{1,0:T(8,128)(2,1)}, u32[]{:S(2)}) copy-start(bf16[128,512]{1,0:T(8,128)(2,1)} %param.10) | copy-start | bytes 393220
  2.6 15.8 %copy-start.8 = (bf16[128,512]{1,0:T(8,128)(2,1)S(1)}, bf16[128,512]{1,0:T(8,128)(2,1)}, u32[]{:S(2)}) copy-start(bf16[128,512]{1,0:T(8,128)(2,1)} %param.11) | copy-start | bytes 393220
  2.6 15.8 %copy-start.10 = (f32[1,128]{1,0:T(1,128)S(1)}, f32[1,128]{1,0:T(1,128)}, u32[]{:S(2)}) copy-start(f32[1,128]{1,0:T(1,128)} %param.13) | copy-start | bytes 1540
  34.1 19.9 %collective-permute-start = (bf16[3,8,8,512]{3,2,0,1:T(8,128)(2,1)S(1)}, bf16[3,8,8,512]{3,2,0,1:T(8,128)(2,1)S(1)}, u32[]{:S(2)}, u32[]{:S(2)}) collective-permute-start(bf16[3,8,8,512]{3,2,0,1:T(8,128)(2,1)S(1)} %fusion.95), channel_id=1, source_target_pairs={{0,16},{16,0},{1,17},{17,1},{2,18},{18,2},{3,19},{19,3},{4,20},{20... | collective-permute-start | bytes 589832 | tf_op jit(solution)/shard_map/ppermute | solution.py:87
  96.6 60.5 %copy-start.1 = (bf16[1,512,512]{2,1,0:T(8,128)(2,1)S(1)}, bf16[1,512,512]{2,1,0:T(8,128)(2,1)}, u32[]{:S(2)}) copy-start(bf16[1,512,512]{2,1,0:T(8,128)(2,1)} %param.14) | copy-start | bytes 1572868
  96.6 60.5 %copy-start.7 = (bf16[128,512]{1,0:T(8,128)(2,1)S(1)}, bf16[128,512]{1,0:T(8,128)(2,1)}, u32[]{:S(2)}) copy-start(bf16[128,512]{1,0:T(8,128)(2,1)} %param.9) | copy-start | bytes 393220
  131.2 26.9 %copy-start.5 = (bf16[1,512,512]{2,1,0:T(8,128)(2,1)S(1)}, bf16[1,512,512]{2,1,0:T(8,128)(2,1)}, u32[]{:S(2)}) copy-start(bf16[1,512,512]{2,1,0:T(8,128)(2,1)} %param.15) | copy-start | bytes 1572868
  145.1 14.8 %collective-permute-start.1 = (bf16[4,8,3,8,512]{4,3,1,0,2:T(8,128)(2,1)S(1)}, bf16[4,8,3,8,512]{4,3,1,0,2:T(8,128)(2,1)}, u32[]{:S(2)}, u32[]{:S(2)}) collective-permute-start(bf16[4,8,3,8,512]{4,3,1,0,2:T(8,128)(2,1)S(1)} %bitcast.153), channel_id=1, source_target_pairs={{0,16},{16,0},{1,17},{17,1},{2,18},{18,2},{3,19},{19,3},{4,20},{20... | collective-permute-start | bytes 2359304 | tf_op jit(solution)/shard_map/ppermute | solution.py:93
  165.6 0.8 copy-start.4
  168.4 1.7 copy-start.3
  173.6 1.7 copy-start.2
  179.7 2.9 %copy-start.11 = (bf16[128,512]{1,0:T(8,128)(2,1)S(1)}, bf16[128,512]{1,0:T(8,128)(2,1)}, u32[]{:S(2)}) copy-start(bf16[128,512]{1,0:T(8,128)(2,1)} %param.12) | copy-start | bytes 393220
  182.6 2.5 %copy-start.12 = (bf16[512,512]{1,0:T(8,128)(2,1)S(1)}, bf16[512,512]{1,0:T(8,128)(2,1)}, u32[]{:S(2)}) copy-start(bf16[512,512]{1,0:T(8,128)(2,1)} %fusion.21) | copy-start | bytes 1572868
  185.1 1.9 copy-start.9
  185.1 1.9 copy-start.13

commit v2 on v1

v2 whole, which is shorter than its diff:
```python
import jax
import jax.numpy as jnp
from jax import lax
from jax.experimental import pallas as pl
from jax.experimental.pallas import tpu as pltpu
from jax.sharding import Mesh
from jax.sharding import PartitionSpec as P

NS_ITERS = 2
FAR, NEAR, CORES, SIDE = 8, 4, 2, 4
VMEM_BYTES = 48 * 1024 * 1024

first_coeff = 3.4445
second_coeff = -4.775
third_coeff = 2.0315
step_scale = 0.5

f32 = jnp.float32
bf16 = jnp.bfloat16
SWAP = [(0, 1), (1, 0)]


def dot(a, b, contract=(1, 0)):
    return lax.dot_general(a, b, ((contract[:1], contract[1:]), ((), ())), preferred_element_type=f32)


def swiglu(gating, lifted):
    return (gating * jax.nn.sigmoid(gating) * lifted).astype(bf16)


def first_kernel(q_ref, gate_ref, up_ref, down_ref, proj_ref, share_ref, gate_t_ref, up_t_ref):
    hidden = swiglu(dot(q_ref[...], gate_ref[0]), dot(q_ref[...], up_ref[0]))
    out = dot(hidden, down_ref[0]).astype(bf16)
    share_ref[...] = dot(out, proj_ref[...]).astype(bf16)
    gate_t_ref[...] = gate_ref[0].T
    up_t_ref[...] = up_ref[0].T


def descent_kernel(place_ref, tokens_ref, gate_ref, up_ref, down_ref, kept_ref, given_ref, sums):
    core, near = place_ref[0], place_ref[1]
    rows = tokens_ref.shape[1] // 2
    part = gate_ref.shape[2] // NEAR
    half = part // CORES
    columns = pl.ds(pl.multiple_of(near * part, part), part)
    keys = jnp.concatenate([tokens_ref[i, :rows] for i in range(NEAR)], axis=0)
    scaled = jnp.concatenate([tokens_ref[i, rows:] for i in range(NEAR)], axis=0)
    gating = dot(gate_ref[0, :, columns].T, keys, (1, 1))
    lifted = dot(up_ref[0, :, columns].T, keys, (1, 1))
    backward = dot(down_ref[0, columns, :], scaled, (1, 1))
    s = jax.nn.sigmoid(gating)
    activated = gating * s
    hidden = (activated * lifted).astype(bf16)
    gate_back = (backward * lifted * s * (1.0 + gating * (1.0 - s))).astype(bf16)
    up_back = (backward * activated).astype(bf16)
    sums[0] = dot(gate_back, keys)
    sums[1] = dot(up_back, keys)
    sums[2] = dot(hidden, scaled)
    mine = pl.ds(pl.multiple_of(core * half, half), half)
    others = pl.ds(pl.multiple_of((1 - core) * half, half), half)
    for m in range(3):
        kept_ref[m * half : (m + 1) * half] = sums[m, mine, :]
        given_ref[m * half : (m + 1) * half] = sums[m, others, :].astype(bf16)


def second_kernel(
    place_ref, own_ref, other_ref, q_ref, gate_t_ref, up_t_ref, down_ref, proj_ref, first_ref, share_ref, work
):
    core = place_ref[0]
    width = q_ref.shape[1]
    part = width // NEAR
    half = part // CORES
    for m in range(3):
        for i in range(NEAR):
            mine = pl.ds(pl.multiple_of(i * part + core * half, half), half)
            others = pl.ds(pl.multiple_of(i * part + (1 - core) * half, half), half)
            work[m, mine, :] = own_ref[i, m * half : (m + 1) * half]
            work[m, others, :] = other_ref[i, m * half : (m + 1) * half]
    for m in range(3):
        widened = work[m].astype(f32)
        magnitude = jnp.sqrt(jnp.sum(widened * widened, keepdims=True)) + 1e-07
        work[m] = (widened / magnitude).astype(bf16)
    for step in range(NS_ITERS):
        for m in range(3):
            current = work[m]
            gram = dot(current, current, (1, 1)).astype(bf16)
            square = dot(gram, gram)
            polynomial = (second_coeff * gram.astype(f32) + third_coeff * square).astype(bf16)
            mixed = dot(polynomial, current)
            work[m] = (first_coeff * current.astype(f32) + mixed).astype(bf16)

    def updated(memory, m):
        return (memory.astype(f32) + step_scale * work[m].astype(f32)).astype(bf16)

    q = q_ref[...]
    gating = dot(q, updated(gate_t_ref[...], 0), (1, 1))
    lifted = dot(q, updated(up_t_ref[...], 1), (1, 1))
    out = dot(swiglu(gating, lifted), updated(down_ref[0], 2)).astype(bf16)
    share_ref[:, :width] = first_ref[...]
    share_ref[:, width:] = dot(out, proj_ref[...]).astype(bf16)


def local(kernel, outs, n_in, scalars, scratch, flops):
    whole = pl.BlockSpec(memory_space=pltpu.VMEM)
    smem = pl.BlockSpec(memory_space=pltpu.SMEM)
    return pl.pallas_call(
        kernel,
        out_shape=[jax.ShapeDtypeStruct(shape, kind) for shape, kind in outs],
        in_specs=[smem] * scalars + [whole] * n_in,
        out_specs=[whole] * len(outs),
        scratch_shapes=scratch,
        compiler_params=pltpu.CompilerParams(vmem_limit_bytes=VMEM_BYTES),
        cost_estimate=pl.CostEstimate(flops=flops, bytes_accessed=3 << 20, transcendentals=0),
    )


def on_device(q_first, keys, values, q_second, rates, gate_memory, up_memory, down_memory, out_proj):
    core = lax.axis_index("core")
    near = lax.axis_index("near")
    place = jnp.stack([core, near]).astype(jnp.int32)
    tokens, width = keys.shape
    unit = width * width

    scaled = (rates[0][:, None] * values.astype(f32)).astype(bf16)
    mine = jnp.concatenate([keys, scaled], axis=0)
    tiles = lax.all_to_all(
        jnp.broadcast_to(mine[None], (NEAR,) + mine.shape), "near", 0, 0, tiled=True
    )
    rows = 3 * width // NEAR // CORES
    kept, given = local(
        descent_kernel,
        [((rows, width), f32), ((rows, width), bf16)],
        4,
        1,
        [pltpu.VMEM((3, width // NEAR, width), f32)],
        12 * tokens * unit,
    )(place, tiles, gate_memory, up_memory, down_memory)
    taken = lax.ppermute(given, "core", SWAP)
    pieces = (kept + taken.astype(f32)).astype(bf16)
    pieces = lax.all_to_all(pieces, "far", 0, 0, tiled=True)
    summed = jnp.sum(pieces.reshape(FAR, -1, width).astype(f32), axis=0).astype(bf16)
    own = lax.all_gather(summed, "far", axis=0, tiled=True)
    own = lax.all_gather(own, "near", axis=0, tiled=False)
    other = lax.ppermute(own, "core", SWAP)
    first_share, gate_t, up_t = local(
        first_kernel,
        [((tokens, width), bf16), ((width, width), bf16), ((width, width), bf16)],
        5,
        0,
        [],
        8 * tokens * unit,
    )(q_first, gate_memory, up_memory, down_memory, out_proj)
    (share,) = local(
        second_kernel,
        [((tokens, 2 * width), bf16)],
        8,
        1,
        [pltpu.VMEM((3, width, width), bf16)],
        36 * width * unit,
    )(place, own, other, q_second, gate_t, up_t, down_memory, out_proj, first_share)
    shares = lax.all_to_all(share, ("x", "y"), 0, 0, tiled=True)
    shares = shares.reshape(SIDE * SIDE, -1, 2 * width)
    return jnp.sum(shares.astype(f32), axis=0).astype(bf16)


def solution(mesh):
    fine = Mesh(
        mesh.devices.reshape(FAR, NEAR, CORES, SIDE, SIDE), ("far", "near", "core", "x", "y")
    )
    seq, head = ("far", "near", "core"), ("x", "y")
    in_specs = (
        P(seq, head),
        P(seq, head),
        P(seq, head),
        P(seq, head),
        P(head, seq),
        P(head, None, None),
        P(head, None, None),
        P(head, None, None),
        P(head, None),
    )
    out_specs = P(seq + head, None)
    return jax.shard_map(
        on_device, mesh=fine, in_specs=in_specs, out_specs=out_specs, check_vma=False
    )
```

time: 203 us -> 177 us (0.87)
  matrix products: 26.3 us -> 0 us
  blocking collectives: 134 us -> 114 us
  waiting for transfers between devices: 1.05 us -> 17 us
  Pallas kernels: 0 us -> 9.68 us
  other arithmetic: 4.73 us -> 1.84 us
  between operations: 2.35 us -> 0.1 us
  local copies, waits for them, and re-layouts: 3.92 us -> 1.73 us
    all_gather x3 -> x1, blocking collectives: 63.2 us -> 33 us  [on_device(): own = lax.all_gather(summed, 'far', axis=0, tiled=True)]
    dot_general x25 -> x0, matrix products: 26.3 us -> none  [dot(): lax.dot_general(a, b, ((contract[:1], contract[1:]), ((), ())), preferred...]
    all_to_all x0 -> x1, waiting for transfers between devices: none -> 14.7 us  [on_device(): lax.all_to_all(jnp.broadcast_to(mine[None], (NEAR,) + mine.shape), 'near'...]
    all_to_all x1, blocking collectives: 42.4 us -> 52.7 us  [on_device(): pieces = lax.all_to_all(pieces, 'far', 0, 0, tiled=True)]
    pallas_call x0 -> x3, Pallas kernels: none -> 9.68 us  [the longest x1 7.41 us: on_device(): local(second_kernel, [((tokens, 2 * width), bf16)], 8, 1, [pltpu.VMEM((3,...]
    all_to_all x0 -> x1, starting transfers between devices: none -> 6.57 us  [on_device(): lax.all_to_all(jnp.broadcast_to(mine[None], (NEAR,) + mine.shape), 'near'...]
    ppermute x1, starting transfers between devices: 18.9 us -> 14.2 us  [on_device(): taken = lax.ppermute(given, 'core', SWAP)]
    unnamed x30 -> x16, local copies, waits for them, and re-layouts: 2.92 us -> 0.68 us
  transfers between devices with their start and end apart: 2 -> 3, of which waited for: 1 -> 3; matrix products, arithmetic and copies ran while one was open for 1% -> 0% of each run, Pallas kernels for 0% -> 0%
where the time goes in v2:
time: 177 us
  blocking collectives  114 us (64%)
  starting transfers between devices  32.5 us (18%)
  waiting for transfers between devices  17 us (10%)
  Pallas kernels  9.68 us (5%)
  other arithmetic  1.84 us (1%)
    all_to_all x1, blocking collectives, on_device(): pieces = lax.all_to_all(pieces, 'far', 0, 0, tiled=True)  52.7 us
    all_gather x1, blocking collectives, on_device(): own = lax.all_gather(summed, 'far', axis=0, tiled=True)  33 us
    all_to_all x1, waiting for transfers between devices, on_device(): lax.all_to_all(jnp.broadcast_to(mine[None], (NEAR,) + mine.shape), 'near'...  14.7 us
    ppermute x1, starting transfers between devices, on_device(): taken = lax.ppermute(given, 'core', SWAP)  14.2 us
    all_gather x1, blocking collectives, on_device(): own = lax.all_gather(own, 'near', axis=0, tiled=False)  14.2 us
    all_to_all x1, blocking collectives, on_device(): shares = lax.all_to_all(share, ('x', 'y'), 0, 0, tiled=True)  14.1 us
    ppermute x1, starting transfers between devices, on_device(): other = lax.ppermute(own, 'core', SWAP)  11.7 us
    pallas_call x1, Pallas kernels, on_device(): local(second_kernel, [((tokens, 2 * width), bf16)], 8, 1, [pltpu.VMEM((3,...  7.41 us
  transfers between devices with their start and end apart: 3, of which 3 were waited for; matrix products, arithmetic and copies ran while one was open for 0% of the time, Pallas kernels for 0%

profile of v2, /device:TPU:1, one launch (start us, length us, event | category | flops | bytes accessed | tf_op | source)
XLA Modules:
  0.0 176.8 jit_solution(11712938457996979390)
XLA Ops:
  0.0 0.0 copy-start.7
  0.0 0.7 copy-done.7
  0.7 0.0 copy-start.6
  0.7 1.0 multiply_convert_fusion
  1.7 0.0 copy-done.6
  1.7 1.0 broadcast_in_dim.2
  2.8 0.0 copy-start
  2.8 0.0 copy-start.1
  2.8 0.0 copy-start.2
  2.8 6.6 %all-to-all-start = ((bf16[4,256,512]{2,1,0:T(8,128)(2,1)}), bf16[4,256,512]{2,1,0:T(8,128)(2,1)S(1)}, u32[]{:S(2)}, u32[]{:S(2)}) async-start(bf16[4,256,512]{2,1,0:T(8,128)(2,1)} %broadcast_in_dim.2), calls=%async_computation | async-start | bytes 2097152 | tf_op jit(solution)/shard_map/all_to_all | solution.py:125
  9.4 0.1 pad_add_fusion.place_ref
  9.4 14.7 %all-to-all-done.tokens_ref = bf16[4,256,512]{2,1,0:T(8,128)(2,1)S(1)} async-done(((bf16[4,256,512]{2,1,0:T(8,128)(2,1)}), bf16[4,256,512]{2,1,0:T(8,128)(2,1)S(1)}, u32[]{:S(2)}, u32[]{:S(2)}) %all-to-all-start) | async-done | bytes 1048608 | tf_op jit(solution)/shard_map/all_to_all | solution.py:125
  24.2 0.0 copy-done
  24.2 0.0 copy-done.1
  24.2 0.0 copy-done.2
  24.2 1.6 shard_map.91
  25.8 14.2 %collective-permute-start = (bf16[192,512]{1,0:T(8,128)(2,1)S(1)}, bf16[192,512]{1,0:T(8,128)(2,1)S(1)}, u32[]{:S(2)}, u32[]{:S(2)}) collective-permute-start(bf16[192,512]{1,0:T(8,128)(2,1)S(1)} %get-tuple-element.11), channel_id=1, source_target_pairs={{0,16},{16,0},{1,17},{17,1},{2,18},{18,2},{3,19},{19,3},{4,20},{20... | collective-permute-start | bytes 589832 | tf_op jit(solution)/shard_map/ppermute | solution.py:137
  40.0 1.0 collective-permute-done
  41.1 52.7 %all_to_all.23 = bf16[8,24,512]{2,1,0:T(8,128)(2,1)S(1)} all-to-all(bf16[8,24,512]{2,1,0:T(8,128)(2,1)S(1)} %bitcast.9), channel_id=1, replica_groups=mesh['far'=8,'near'=4,'core'=2,'x'=4,'y'=4] {'far'}, dimensions={0} | all-to-all | bytes 393216 | tf_op jit(solution)/shard_map/all_to_all | solution.py:139
  93.8 33.0 %all_gather.9 = bf16[192,512]{1,0:T(8,128)(2,1)S(1)} all-gather(bf16[24,512]{1,0:T(8,128)(2,1)S(1)} %reduce_sum.24), channel_id=1, replica_groups=mesh['far'=8,'near'=4,'core'=2,'x'=4,'y'=4] {'far'}, dimensions={0}, use_global_device_ids=true | all-gather | bytes 221184 | tf_op jit(solution)/shard_map/all_gather | solution.py:141
  126.8 0.0 copy-start.3
  126.8 0.0 copy-start.4
  126.8 14.2 %all-gather = bf16[768,512]{1,0:T(8,128)(2,1)S(1)} all-gather(bf16[192,512]{1,0:T(8,128)(2,1)S(1)} %all_gather.9), channel_id=2, replica_groups=mesh['far'=8,'near'=4,'core'=2,'x'=4,'y'=4] {'near'}, dimensions={0}, use_global_device_ids=true | all-gather | bytes 983040 | tf_op jit(solution)/shard_map/all_gather | solution.py:142
  141.0 11.7 %collective-permute-start.1 = (bf16[4,192,512]{2,1,0:T(8,128)(2,1)S(1)}, bf16[4,192,512]{2,1,0:T(8,128)(2,1)S(1)}, u32[]{:S(2)}, u32[]{:S(2)}) collective-permute-start(bf16[4,192,512]{2,1,0:T(8,128)(2,1)S(1)} %bitcast.6), channel_id=1, source_target_pairs={{0,16},{16,0},{1,17},{17,1},{2,18},{18,2},{3,19},{19,3},{4,20},{20... | collective-permute-start | bytes 2359304 | tf_op jit(solution)/shard_map/ppermute | solution.py:143
  152.7 0.0 copy-done.3
  152.7 0.0 copy-done.4
  152.7 0.7 shard_map.92
  153.4 1.2 collective-permute-done.1.other_ref
  154.6 0.0 copy-done.5
  154.6 7.4 %shard_map.93 = bf16[128,1024]{1,0:T(8,128)(2,1)S(1)} custom-call(s32[2]{0:T(128)S(1)} %pad_add_fusion.place_ref, bf16[4,192,512]{2,1,0:T(8,128)(2,1)S(1)} %bitcast.7, bf16[4,192,512]{2,1,0:T(8,128)(2,1)S(1)} %collective-permute-done.1.other_ref, bf16[128,512]{1,0:T(8,128)(2,1)S(1)} %copy-done.5, bf16[512,512]{1,0:T(8,128)(2,1)S(1)} %get-tuple-element.12.gate_t_ref, ...), custom_call_target="tpu_custom_call" | custom-call | flops 4831838208 | bytes 3145728 | tf_op jit(solution)/shard_map/pallas_call | solution.py:152
  162.0 14.1 %all_to_all.24 = bf16[16,8,1024]{2,1,0:T(8,128)(2,1)S(1)} all-to-all(bf16[16,8,1024]{2,1,0:T(8,128)(2,1)S(1)} %bitcast.8), channel_id=1, replica_groups=mesh['far'=8,'near'=4,'core'=2,'x'=4,'y'=4] {'x','y'}, dimensions={0} | all-to-all | bytes 524288 | tf_op jit(solution)/shard_map/all_to_all | solution.py:160
  176.1 0.6 reduce_sum.25
  (4 shorter events, 0.1 us)
Async XLA Ops:
  0.0 0.7 copy-start.7
  0.7 1.0 copy-start.6
  2.8 21.4 %copy-start = (bf16[1,512,512]{2,1,0:T(8,128)(2,1)S(1)}, bf16[1,512,512]{2,1,0:T(8,128)(2,1)}, u32[]{:S(2)}) copy-start(bf16[1,512,512]{2,1,0:T(8,128)(2,1)} %gate_ref.3) | copy-start | bytes 1572868
  2.8 21.4 %copy-start.1 = (bf16[1,512,512]{2,1,0:T(8,128)(2,1)S(1)}, bf16[1,512,512]{2,1,0:T(8,128)(2,1)}, u32[]{:S(2)}) copy-start(bf16[1,512,512]{2,1,0:T(8,128)(2,1)} %up_ref.3) | copy-start | bytes 1572868
  2.8 21.4 %copy-start.2 = (bf16[1,512,512]{2,1,0:T(8,128)(2,1)S(1)}, bf16[1,512,512]{2,1,0:T(8,128)(2,1)}, u32[]{:S(2)}) copy-start(bf16[1,512,512]{2,1,0:T(8,128)(2,1)} %down_ref.5) | copy-start | bytes 1572868
  2.8 21.4 %all-to-all-start = ((bf16[4,256,512]{2,1,0:T(8,128)(2,1)}), bf16[4,256,512]{2,1,0:T(8,128)(2,1)S(1)}, u32[]{:S(2)}, u32[]{:S(2)}) async-start(bf16[4,256,512]{2,1,0:T(8,128)(2,1)} %broadcast_in_dim.2), calls=%async_computation | async-start | bytes 2097152 | tf_op jit(solution)/shard_map/all_to_all | solution.py:125
  25.8 15.3 %collective-permute-start = (bf16[192,512]{1,0:T(8,128)(2,1)S(1)}, bf16[192,512]{1,0:T(8,128)(2,1)S(1)}, u32[]{:S(2)}, u32[]{:S(2)}) collective-permute-start(bf16[192,512]{1,0:T(8,128)(2,1)S(1)} %get-tuple-element.11), channel_id=1, source_target_pairs={{0,16},{16,0},{1,17},{17,1},{2,18},{18,2},{3,19},{19,3},{4,20},{20... | collective-permute-start | bytes 589832 | tf_op jit(solution)/shard_map/ppermute | solution.py:137
  126.8 25.9 %copy-start.3 = (bf16[512,512]{1,0:T(8,128)(2,1)S(1)}, bf16[512,512]{1,0:T(8,128)(2,1)}, u32[]{:S(2)}) copy-start(bf16[512,512]{1,0:T(8,128)(2,1)} %proj_ref.3) | copy-start | bytes 1572868
  126.8 26.0 %copy-start.4 = (bf16[128,512]{1,0:T(8,128)(2,1)S(1)}, bf16[128,512]{1,0:T(8,128)(2,1)}, u32[]{:S(2)}) copy-start(bf16[128,512]{1,0:T(8,128)(2,1)} %q_ref.2) | copy-start | bytes 393220
  141.0 13.6 %copy-start.5 = (bf16[128,512]{1,0:T(8,128)(2,1)S(1)}, bf16[128,512]{1,0:T(8,128)(2,1)}, u32[]{:S(2)}) copy-start(bf16[128,512]{1,0:T(8,128)(2,1)} %q_ref.3) | copy-start | bytes 393220
  141.0 13.6 %collective-permute-start.1 = (bf16[4,192,512]{2,1,0:T(8,128)(2,1)S(1)}, bf16[4,192,512]{2,1,0:T(8,128)(2,1)S(1)}, u32[]{:S(2)}, u32[]{:S(2)}) collective-permute-start(bf16[4,192,512]{2,1,0:T(8,128)(2,1)S(1)} %bitcast.6), channel_id=1, source_target_pairs={{0,16},{16,0},{1,17},{17,1},{2,18},{18,2},{3,19},{19,3},{4,20},{20... | collective-permute-start | bytes 2359304 | tf_op jit(solution)/shard_map/ppermute | solution.py:143

commit v3 on v2

--- a/solution.py
+++ b/solution.py
@@ -7,7 +7,7 @@
 from jax.sharding import PartitionSpec as P
 
 NS_ITERS = 2
-FAR, NEAR, CORES, SIDE = 8, 4, 2, 4
+FAR, MID, PAIR, CORES, SIDE = 4, 4, 2, 2, 4
 VMEM_BYTES = 48 * 1024 * 1024
 
 first_coeff = 3.4445
@@ -36,17 +36,18 @@
     up_t_ref[...] = up_ref[0].T
 
 
-def descent_kernel(place_ref, tokens_ref, gate_ref, up_ref, down_ref, kept_ref, given_ref, sums):
-    core, near = place_ref[0], place_ref[1]
-    rows = tokens_ref.shape[1] // 2
-    part = gate_ref.shape[2] // NEAR
+def descent_kernel(
+    place_ref, keys_a, keys_b, scaled_a, scaled_b, gate_t_ref, up_t_ref, down_ref, kept_ref, given_ref, sums
+):
+    core, pair = place_ref[0], place_ref[1]
+    part = down_ref.shape[1] // PAIR
     half = part // CORES
-    columns = pl.ds(pl.multiple_of(near * part, part), part)
-    keys = jnp.concatenate([tokens_ref[i, :rows] for i in range(NEAR)], axis=0)
-    scaled = jnp.concatenate([tokens_ref[i, rows:] for i in range(NEAR)], axis=0)
-    gating = dot(gate_ref[0, :, columns].T, keys, (1, 1))
-    lifted = dot(up_ref[0, :, columns].T, keys, (1, 1))
-    backward = dot(down_ref[0, columns, :], scaled, (1, 1))
+    units = pl.ds(pl.multiple_of(pair * part, part), part)
+    keys = jnp.concatenate([keys_a[...], keys_b[...]], axis=0)
+    scaled = jnp.concatenate([scaled_a[...], scaled_b[...]], axis=0)
+    gating = dot(gate_t_ref[units, :], keys, (1, 1))
+    lifted = dot(up_t_ref[units, :], keys, (1, 1))
+    backward = dot(down_ref[0, units, :], scaled, (1, 1))
     s = jax.nn.sigmoid(gating)
     activated = gating * s
     hidden = (activated * lifted).astype(bf16)
@@ -63,18 +64,18 @@
 
 
 def second_kernel(
-    place_ref, own_ref, other_ref, q_ref, gate_t_ref, up_t_ref, down_ref, proj_ref, first_ref, share_ref, work
+    place_ref, a_ref, b_ref, c_ref, d_ref, q_ref, gate_t_ref, up_t_ref, down_ref, proj_ref, first_ref, share_ref, work
 ):
-    core = place_ref[0]
+    core, pair = place_ref[0], place_ref[1]
     width = q_ref.shape[1]
-    part = width // NEAR
+    part = width // PAIR
     half = part // CORES
-    for m in range(3):
-        for i in range(NEAR):
-            mine = pl.ds(pl.multiple_of(i * part + core * half, half), half)
-            others = pl.ds(pl.multiple_of(i * part + (1 - core) * half, half), half)
-            work[m, mine, :] = own_ref[i, m * half : (m + 1) * half]
-            work[m, others, :] = other_ref[i, m * half : (m + 1) * half]
+    for ref, other_pair, other_core in ((a_ref, 0, 0), (b_ref, 1, 0), (c_ref, 0, 1), (d_ref, 1, 1)):
+        at_pair = 1 - pair if other_pair else pair
+        at_core = 1 - core if other_core else core
+        at = pl.ds(pl.multiple_of(at_pair * part + at_core * half, half), half)
+        for m in range(3):
+            work[m, at, :] = ref[m * half : (m + 1) * half]
     for m in range(3):
         widened = work[m].astype(f32)
         magnitude = jnp.sqrt(jnp.sum(widened * widened, keepdims=True)) + 1e-07
@@ -115,32 +116,14 @@
 
 def on_device(q_first, keys, values, q_second, rates, gate_memory, up_memory, down_memory, out_proj):
     core = lax.axis_index("core")
-    near = lax.axis_index("near")
-    place = jnp.stack([core, near]).astype(jnp.int32)
+    pair = lax.axis_index("pair")
+    place = jnp.stack([core, pair]).astype(jnp.int32)
     tokens, width = keys.shape
     unit = width * width
 
+    keys_next = lax.ppermute(keys, "pair", SWAP)
     scaled = (rates[0][:, None] * values.astype(f32)).astype(bf16)
-    mine = jnp.concatenate([keys, scaled], axis=0)
-    tiles = lax.all_to_all(
-        jnp.broadcast_to(mine[None], (NEAR,) + mine.shape), "near", 0, 0, tiled=True
-    )
-    rows = 3 * width // NEAR // CORES
-    kept, given = local(
-        descent_kernel,
-        [((rows, width), f32), ((rows, width), bf16)],
-        4,
-        1,
-        [pltpu.VMEM((3, width // NEAR, width), f32)],
-        12 * tokens * unit,
-    )(place, tiles, gate_memory, up_memory, down_memory)
-    taken = lax.ppermute(given, "core", SWAP)
-    pieces = (kept + taken.astype(f32)).astype(bf16)
-    pieces = lax.all_to_all(pieces, "far", 0, 0, tiled=True)
-    summed = jnp.sum(pieces.reshape(FAR, -1, width).astype(f32), axis=0).astype(bf16)
-    own = lax.all_gather(summed, "far", axis=0, tiled=True)
-    own = lax.all_gather(own, "near", axis=0, tiled=False)
-    other = lax.ppermute(own, "core", SWAP)
+    scaled_next = lax.ppermute(scaled, "pair", SWAP)
     first_share, gate_t, up_t = local(
         first_kernel,
         [((tokens, width), bf16), ((width, width), bf16), ((width, width), bf16)],
@@ -149,14 +132,35 @@
         [],
         8 * tokens * unit,
     )(q_first, gate_memory, up_memory, down_memory, out_proj)
+    rows = 3 * width // PAIR // CORES
+    kept, given = local(
+        descent_kernel,
+        [((rows, width), f32), ((rows, width), bf16)],
+        7,
+        1,
+        [pltpu.VMEM((3, width // PAIR, width), f32)],
+        12 * tokens * unit,
+    )(place, keys, keys_next, scaled, scaled_next, gate_t, up_t, down_memory)
+    taken = lax.ppermute(given, "core", SWAP)
+    pieces = (kept + taken.astype(f32)).astype(bf16)
+    pieces = lax.all_to_all(pieces, "mid", 0, 0, tiled=True).reshape(MID, -1, width)
+    summed = jnp.sum(pieces.astype(f32), axis=0).astype(bf16)
+    groups = lax.all_gather(summed, "far", axis=0, tiled=False)
+    summed = jnp.sum(groups.astype(f32), axis=0).astype(bf16)
+    part_a = lax.all_to_all(
+        jnp.broadcast_to(summed[None], (MID,) + summed.shape), "mid", 0, 0, tiled=True
+    ).reshape(rows, width)
+    part_b = lax.ppermute(part_a, "pair", SWAP)
+    part_c = lax.ppermute(part_a, "core", SWAP)
+    part_d = lax.ppermute(part_b, "core", SWAP)
     (share,) = local(
         second_kernel,
         [((tokens, 2 * width), bf16)],
-        8,
+        10,
         1,
         [pltpu.VMEM((3, width, width), bf16)],
         36 * width * unit,
-    )(place, own, other, q_second, gate_t, up_t, down_memory, out_proj, first_share)
+    )(place, part_a, part_b, part_c, part_d, q_second, gate_t, up_t, down_memory, out_proj, first_share)
     shares = lax.all_to_all(share, ("x", "y"), 0, 0, tiled=True)
     shares = shares.reshape(SIDE * SIDE, -1, 2 * width)
     return jnp.sum(shares.astype(f32), axis=0).astype(bf16)
@@ -164,9 +168,10 @@
 
 def solution(mesh):
     fine = Mesh(
-        mesh.devices.reshape(FAR, NEAR, CORES, SIDE, SIDE), ("far", "near", "core", "x", "y")
+        mesh.devices.reshape(FAR, MID, PAIR, CORES, SIDE, SIDE),
+        ("far", "mid", "pair", "core", "x", "y"),
     )
-    seq, head = ("far", "near", "core"), ("x", "y")
+    seq, head = ("far", "mid", "pair", "core"), ("x", "y")
     in_specs = (
         P(seq, head),
         P(seq, head),

time: 177 us -> 165 us (0.932)
  waiting for transfers between devices: 17 us -> 8.47 us
  blocking collectives: 114 us -> 107 us
  local copies, waits for them, and re-layouts: 1.73 us -> 5.15 us
    all_to_all x1 -> x0, waiting for transfers between devices: 14.7 us -> none  [on_device(): lax.all_to_all(jnp.broadcast_to(mine[None], (NEAR,) + mine.shape), 'near'...]
    all_to_all x1 -> x0, starting transfers between devices: 6.57 us -> none  [on_device(): lax.all_to_all(jnp.broadcast_to(mine[None], (NEAR,) + mine.shape), 'near'...]
    ppermute x1 -> x5, waiting for transfers between devices: 1.21 us -> 7.14 us  [the longest x1 5.82 us: on_device(): part_b = lax.ppermute(part_a, 'pair', SWAP)]
    unnamed x16 -> x20, local copies, waits for them, and re-layouts: 0.68 us -> 5.12 us
    ppermute x1 -> x5, starting transfers between devices: 11.7 us -> 15.8 us  [the longest x1 4.38 us: on_device(): scaled_next = lax.ppermute(scaled, 'pair', SWAP)]
    all_gather x2 -> x1, blocking collectives: 47.2 us -> 44.2 us  [on_device(): groups = lax.all_gather(summed, 'far', axis=0, tiled=False)]
    all_to_all x1 -> x2, blocking collectives: 52.7 us -> 50.6 us  [the longest x1 25.4 us: on_device(): lax.all_to_all(pieces, 'mid', 0, 0, tiled=True).reshape(MID, -1, width)]
  transfers between devices with their start and end apart: 3 -> 6, of which waited for: 3 -> 3; matrix products, arithmetic and copies ran while one was open for 0% -> 0% of each run, Pallas kernels for 0% -> 0%
where the time goes in v3:
time: 165 us; the launch traced here: 164 us
  blocking collectives  107 us (65%)
  starting transfers between devices  31.4 us (19%)
  Pallas kernels  9.53 us (6%)
  waiting for transfers between devices  8.47 us (5%)
  local copies, waits for them, and re-layouts  5.15 us (3%)
  other arithmetic  2 us (1%)
    all_gather x1, blocking collectives, on_device(): groups = lax.all_gather(summed, 'far', axis=0, tiled=False)  44.2 us
    all_to_all x1, blocking collectives, on_device(): lax.all_to_all(pieces, 'mid', 0, 0, tiled=True).reshape(MID, -1, width)  25.4 us
    all_to_all x1, blocking collectives, on_device(): lax.all_to_all(jnp.broadcast_to(summed[None], (MID,) + summed.shape), 'mi...  25.2 us
    ppermute x1, starting transfers between devices, on_device(): taken = lax.ppermute(given, 'core', SWAP)  15.6 us
    all_to_all x1, blocking collectives, on_device(): shares = lax.all_to_all(share, ('x', 'y'), 0, 0, tiled=True)  12.6 us
    pallas_call x1, Pallas kernels, on_device(): local(second_kernel, [((tokens, 2 * width), bf16)], 10, 1, [pltpu.VMEM((3...  7.42 us
    ppermute x1, waiting for transfers between devices, on_device(): part_b = lax.ppermute(part_a, 'pair', SWAP)  5.82 us
    unnamed x20, local copies, waits for them, and re-layouts  5.12 us
  transfers between devices with their start and end apart: 6, of which 3 were waited for; matrix products, arithmetic and copies ran while one was open for 0% of the time, Pallas kernels for 0%

profile of v3, /device:TPU:1, one launch (start us, length us, event | category | flops | bytes accessed | tf_op | source)
XLA Modules:
  0.0 164.1 jit_solution(17655295952814150185)
XLA Ops:
  0.0 0.7 copy-done.9
  0.7 1.0 multiply_convert_fusion.scaled_a
  1.7 4.4 %collective-permute-start.1 = (bf16[128,512]{1,0:T(8,128)(2,1)S(1)}, bf16[128,512]{1,0:T(8,128)(2,1)S(1)}, u32[]{:S(2)}, u32[]{:S(2)}) collective-permute-start(bf16[128,512]{1,0:T(8,128)(2,1)S(1)} %multiply_convert_fusion.scaled_a), channel_id=1, source_target_pairs={{0,32},{32,0},{1,33},{33,1},{2,34},{34,2},{3,35},{35,3},{4,36},{36... | collective-permute-start | bytes 393224 | tf_op jit(solution)/shard_map/ppermute | solution.py:126
  6.1 1.9 %collective-permute-start = (bf16[128,512]{1,0:T(8,128)(2,1)S(1)}, bf16[128,512]{1,0:T(8,128)(2,1)S(1)}, u32[]{:S(2)}, u32[]{:S(2)}) collective-permute-start(bf16[128,512]{1,0:T(8,128)(2,1)S(1)} %copy-done.7), channel_id=1, source_target_pairs={{0,32},{32,0},{1,33},{33,1},{2,34},{34,2},{3,35},{35,3},{4,36},{36... | collective-permute-start | bytes 393224 | tf_op jit(solution)/shard_map/ppermute | solution.py:124
  8.0 0.0 copy-start
  8.0 1.0 copy-done
  9.1 1.0 copy-done.2
  10.1 1.0 copy-done.3
  11.2 1.0 copy-done.4
  12.2 0.7 shard_map.91
  12.9 0.1 pad_add_fusion.place_ref
  13.0 0.0 collective-permute-done.1.scaled_b
  13.0 0.3 copy-done.1
  13.2 1.4 shard_map.92
  14.7 15.6 %collective-permute-start.2 = (bf16[384,512]{1,0:T(8,128)(2,1)S(1)}, bf16[384,512]{1,0:T(8,128)(2,1)S(1)}, u32[]{:S(2)}, u32[]{:S(2)}) collective-permute-start(bf16[384,512]{1,0:T(8,128)(2,1)S(1)} %get-tuple-element.13), channel_id=1, source_target_pairs={{0,16},{16,0},{1,17},{17,1},{2,18},{18,2},{3,19},{19,3},{4,20},{20... | collective-permute-start | bytes 1179656 | tf_op jit(solution)/shard_map/ppermute | solution.py:144
  30.3 1.3 collective-permute-done.2
  31.7 0.1 add_convert_fusion
  31.8 25.4 %all_to_all.23 = bf16[4,96,512]{2,1,0:T(8,128)(2,1)S(1)} all-to-all(bf16[4,96,512]{2,1,0:T(8,128)(2,1)S(1)} %bitcast.11), channel_id=1, replica_groups=mesh['far'=4,'mid'=4,'pair'=2,'core'=2,'x'=4,'y'=4] {'mid'}, dimensions={0} | all-to-all | bytes 786432 | tf_op jit(solution)/shard_map/all_to_all | solution.py:146
  57.2 0.1 reduce_sum.36
  57.3 44.2 %all-gather = bf16[384,512]{1,0:T(8,128)(2,1)S(1)} all-gather(bf16[96,512]{1,0:T(8,128)(2,1)S(1)} %reduce_sum.36), channel_id=2, replica_groups=mesh['far'=4,'mid'=4,'pair'=2,'core'=2,'x'=4,'y'=4] {'far'}, dimensions={0}, use_global_device_ids=true | all-gather | bytes 491520 | tf_op jit(solution)/shard_map/all_gather | solution.py:148
  101.5 0.1 reduce_sum.37
  101.6 0.0 copy-start.5
  101.6 0.0 copy-start.8
  101.7 25.2 %all_to_all.24 = bf16[4,96,512]{2,1,0:T(8,128)(2,1)S(1)} all-to-all(bf16[4,96,512]{2,1,0:T(8,128)(2,1)S(1)} %broadcast_in_dim.2), channel_id=1, replica_groups=mesh['far'=4,'mid'=4,'pair'=2,'core'=2,'x'=4,'y'=4] {'mid'}, dimensions={0} | all-to-all | bytes 786432 | tf_op jit(solution)/shard_map/all_to_all | solution.py:150
  126.8 1.9 %collective-permute-start.3 = (bf16[384,512]{1,0:T(8,128)(2,1)S(1)}, bf16[384,512]{1,0:T(8,128)(2,1)S(1)}, u32[]{:S(2)}, u32[]{:S(2)}) collective-permute-start(bf16[384,512]{1,0:T(8,128)(2,1)S(1)} %bitcast.7), channel_id=1, source_target_pairs={{0,32},{32,0},{1,33},{33,1},{2,34},{34,2},{3,35},{35,3},{4,36},{36... | collective-permute-start | bytes 1179656 | tf_op jit(solution)/shard_map/ppermute | solution.py:153
  128.7 3.3 %collective-permute-start.4 = (bf16[384,512]{1,0:T(8,128)(2,1)S(1)}, bf16[384,512]{1,0:T(8,128)(2,1)S(1)}, u32[]{:S(2)}, u32[]{:S(2)}) collective-permute-start(bf16[384,512]{1,0:T(8,128)(2,1)S(1)} %bitcast.8), channel_id=1, source_target_pairs={{0,16},{16,0},{1,17},{17,1},{2,18},{18,2},{3,19},{19,3},{4,20},{20... | collective-permute-start | bytes 1179656 | tf_op jit(solution)/shard_map/ppermute | solution.py:154
  132.1 5.8 %collective-permute-done.3.b_ref = bf16[384,512]{1,0:T(8,128)(2,1)S(1)} collective-permute-done((bf16[384,512]{1,0:T(8,128)(2,1)S(1)}, bf16[384,512]{1,0:T(8,128)(2,1)S(1)}, u32[]{:S(2)}, u32[]{:S(2)}) %collective-permute-start.3) | collective-permute-done | bytes 393248 | tf_op jit(solution)/shard_map/ppermute | solution.py:153
  137.9 4.2 %collective-permute-start.5 = (bf16[384,512]{1,0:T(8,128)(2,1)S(1)}, bf16[384,512]{1,0:T(8,128)(2,1)S(1)}, u32[]{:S(2)}, u32[]{:S(2)}) collective-permute-start(bf16[384,512]{1,0:T(8,128)(2,1)S(1)} %collective-permute-done.3.b_ref), channel_id=1, source_target_pairs={{0,16},{16,0},{1,17},{17,1},{2,18},{18,2},{3,19},{19,3},{4,20},{20... | collective-permute-start | bytes 1179656 | tf_op jit(solution)/shard_map/ppermute | solution.py:155
  142.2 1.3 collective-permute-done.5.d_ref
  143.5 7.4 %shard_map.93 = bf16[128,1024]{1,0:T(8,128)(2,1)S(1)} custom-call(s32[2]{0:T(128)S(1)} %pad_add_fusion.place_ref, bf16[384,512]{1,0:T(8,128)(2,1)S(1)} %bitcast.9, bf16[384,512]{1,0:T(8,128)(2,1)S(1)} %collective-permute-done.3.b_ref, bf16[384,512]{1,0:T(8,128)(2,1)S(1)} %collective-permute-done.4.c_ref, bf16[384,512]{1,0:T(8,128)(2,1)S(1)} %collective-permute-done.5.d_ref, ...), custom_call_target="tpu_custom_call" | custom-call | flops 4831838208 | bytes 3145728 | tf_op jit(solution)/shard_map/pallas_call | solution.py:156
  150.9 12.6 %all_to_all.25 = bf16[16,8,1024]{2,1,0:T(8,128)(2,1)S(1)} all-to-all(bf16[16,8,1024]{2,1,0:T(8,128)(2,1)S(1)} %bitcast.10), channel_id=1, replica_groups=mesh['far'=4,'mid'=4,'pair'=2,'core'=2,'x'=4,'y'=4] {'x','y'}, dimensions={0} | all-to-all | bytes 524288 | tf_op jit(solution)/shard_map/all_to_all | solution.py:164
  163.5 0.6 reduce_sum.38
  (14 shorter events, 0.1 us)
Async XLA Ops:
  0.0 0.7 copy-start.9
  0.7 5.4 %copy-start.7 = (bf16[128,512]{1,0:T(8,128)(2,1)S(1)}, bf16[128,512]{1,0:T(8,128)(2,1)}, u32[]{:S(2)}) copy-start(bf16[128,512]{1,0:T(8,128)(2,1)} %keys_a.1) | copy-start | bytes 393220
  0.7 7.4 %copy-start.6 = (bf16[128,512]{1,0:T(8,128)(2,1)S(1)}, bf16[128,512]{1,0:T(8,128)(2,1)}, u32[]{:S(2)}) copy-start(bf16[128,512]{1,0:T(8,128)(2,1)} %q_ref.2) | copy-start | bytes 393220
  1.7 11.3 %collective-permute-start.1 = (bf16[128,512]{1,0:T(8,128)(2,1)S(1)}, bf16[128,512]{1,0:T(8,128)(2,1)S(1)}, u32[]{:S(2)}, u32[]{:S(2)}) collective-permute-start(bf16[128,512]{1,0:T(8,128)(2,1)S(1)} %multiply_convert_fusion.scaled_a), channel_id=1, source_target_pairs={{0,32},{32,0},{1,33},{33,1},{2,34},{34,2},{3,35},{35,3},{4,36},{36... | collective-permute-start | bytes 393224 | tf_op jit(solution)/shard_map/ppermute | solution.py:126
  6.1 6.9 %collective-permute-start = (bf16[128,512]{1,0:T(8,128)(2,1)S(1)}, bf16[128,512]{1,0:T(8,128)(2,1)S(1)}, u32[]{:S(2)}, u32[]{:S(2)}) collective-permute-start(bf16[128,512]{1,0:T(8,128)(2,1)S(1)} %copy-done.7), channel_id=1, source_target_pairs={{0,32},{32,0},{1,33},{33,1},{2,34},{34,2},{3,35},{35,3},{4,36},{36... | collective-permute-start | bytes 393224 | tf_op jit(solution)/shard_map/ppermute | solution.py:124
  8.0 1.0 copy-start
  9.1 1.0 copy-start.2
  10.1 1.0 copy-start.3
  11.2 1.0 copy-start.4
  12.2 1.0 copy-start.1
  14.7 16.9 %collective-permute-start.2 = (bf16[384,512]{1,0:T(8,128)(2,1)S(1)}, bf16[384,512]{1,0:T(8,128)(2,1)S(1)}, u32[]{:S(2)}, u32[]{:S(2)}) collective-permute-start(bf16[384,512]{1,0:T(8,128)(2,1)S(1)} %get-tuple-element.13), channel_id=1, source_target_pairs={{0,16},{16,0},{1,17},{17,1},{2,18},{18,2},{3,19},{19,3},{4,20},{20... | collective-permute-start | bytes 1179656 | tf_op jit(solution)/shard_map/ppermute | solution.py:144
  101.6 41.9 %copy-start.5 = (bf16[512,512]{1,0:T(8,128)(2,1)S(1)}, bf16[512,512]{1,0:T(8,128)(2,1)}, u32[]{:S(2)}) copy-start(bf16[512,512]{1,0:T(8,128)(2,1)} %proj_ref.3) | copy-start | bytes 1572868
  101.6 41.8 %copy-start.8 = (bf16[128,512]{1,0:T(8,128)(2,1)S(1)}, bf16[128,512]{1,0:T(8,128)(2,1)}, u32[]{:S(2)}) copy-start(bf16[128,512]{1,0:T(8,128)(2,1)} %q_ref.3) | copy-start | bytes 393220
  126.8 11.1 %collective-permute-start.3 = (bf16[384,512]{1,0:T(8,128)(2,1)S(1)}, bf16[384,512]{1,0:T(8,128)(2,1)S(1)}, u32[]{:S(2)}, u32[]{:S(2)}) collective-permute-start(bf16[384,512]{1,0:T(8,128)(2,1)S(1)} %bitcast.7), channel_id=1, source_target_pairs={{0,32},{32,0},{1,33},{33,1},{2,34},{34,2},{3,35},{35,3},{4,36},{36... | collective-permute-start | bytes 1179656 | tf_op jit(solution)/shard_map/ppermute | solution.py:153
  128.7 13.4 %collective-permute-start.4 = (bf16[384,512]{1,0:T(8,128)(2,1)S(1)}, bf16[384,512]{1,0:T(8,128)(2,1)S(1)}, u32[]{:S(2)}, u32[]{:S(2)}) collective-permute-start(bf16[384,512]{1,0:T(8,128)(2,1)S(1)} %bitcast.8), channel_id=1, source_target_pairs={{0,16},{16,0},{1,17},{17,1},{2,18},{18,2},{3,19},{19,3},{4,20},{20... | collective-permute-start | bytes 1179656 | tf_op jit(solution)/shard_map/ppermute | solution.py:154
  137.9 5.6 %collective-permute-start.5 = (bf16[384,512]{1,0:T(8,128)(2,1)S(1)}, bf16[384,512]{1,0:T(8,128)(2,1)S(1)}, u32[]{:S(2)}, u32[]{:S(2)}) collective-permute-start(bf16[384,512]{1,0:T(8,128)(2,1)S(1)} %collective-permute-done.3.b_ref), channel_id=1, source_target_pairs={{0,16},{16,0},{1,17},{17,1},{2,18},{18,2},{3,19},{19,3},{4,20},{20... | collective-permute-start | bytes 1179656 | tf_op jit(solution)/shard_map/ppermute | solution.py:155

commit v4 on v3

--- a/solution.py
+++ b/solution.py
@@ -1,3 +1,5 @@
+import math
+
 import jax
 import jax.numpy as jnp
 from jax import lax
@@ -7,7 +9,7 @@
 from jax.sharding import PartitionSpec as P
 
 NS_ITERS = 2
-FAR, MID, PAIR, CORES, SIDE = 4, 4, 2, 2, 4
+FAR, HIGH, LOW, PAIR, CORES, SIDE = 4, 2, 2, 2, 2, 4
 VMEM_BYTES = 48 * 1024 * 1024
 
 first_coeff = 3.4445
@@ -64,18 +66,23 @@
 
 
 def second_kernel(
-    place_ref, a_ref, b_ref, c_ref, d_ref, q_ref, gate_t_ref, up_t_ref, down_ref, proj_ref, first_ref, share_ref, work
+    place_ref, own_ref, other_ref, q_ref, gate_t_ref, up_t_ref, down_ref, proj_ref, first_ref, share_ref, work
 ):
-    core, pair = place_ref[0], place_ref[1]
+    core = place_ref[0]
     width = q_ref.shape[1]
-    part = width // PAIR
-    half = part // CORES
-    for ref, other_pair, other_core in ((a_ref, 0, 0), (b_ref, 1, 0), (c_ref, 0, 1), (d_ref, 1, 1)):
-        at_pair = 1 - pair if other_pair else pair
-        at_core = 1 - core if other_core else core
-        at = pl.ds(pl.multiple_of(at_pair * part + at_core * half, half), half)
-        for m in range(3):
-            work[m, at, :] = ref[m * half : (m + 1) * half]
+    half = width // PAIR // CORES
+    piece = 3 * half // LOW
+    step = math.gcd(piece, half)
+    for low in range(LOW):
+        for pair in range(PAIR):
+            for row in range(0, piece, step):
+                m, line = divmod(low * piece + row, half)
+                base = pair * CORES * half + line
+                mine = pl.multiple_of(base + core * half, step)
+                others = pl.multiple_of(base + (1 - core) * half, step)
+                at = (low * PAIR + pair) * piece + row
+                work[m, pl.ds(mine, step), :] = own_ref[at : at + step]
+                work[m, pl.ds(others, step), :] = other_ref[at : at + step]
     for m in range(3):
         widened = work[m].astype(f32)
         magnitude = jnp.sqrt(jnp.sum(widened * widened, keepdims=True)) + 1e-07
@@ -141,26 +148,24 @@
         [pltpu.VMEM((3, width // PAIR, width), f32)],
         12 * tokens * unit,
     )(place, keys, keys_next, scaled, scaled_next, gate_t, up_t, down_memory)
-    taken = lax.ppermute(given, "core", SWAP)
+    taken = lax.all_gather(given, "core", axis=0, tiled=False)
+    taken = lax.dynamic_index_in_dim(taken, 1 - core, 0, keepdims=False)
     pieces = (kept + taken.astype(f32)).astype(bf16)
-    pieces = lax.all_to_all(pieces, "mid", 0, 0, tiled=True).reshape(MID, -1, width)
+    pieces = lax.all_to_all(pieces, ("low", "high"), 0, 0, tiled=True).reshape(HIGH * LOW, -1, width)
     summed = jnp.sum(pieces.astype(f32), axis=0).astype(bf16)
-    groups = lax.all_gather(summed, "far", axis=0, tiled=False)
-    summed = jnp.sum(groups.astype(f32), axis=0).astype(bf16)
-    part_a = lax.all_to_all(
-        jnp.broadcast_to(summed[None], (MID,) + summed.shape), "mid", 0, 0, tiled=True
-    ).reshape(rows, width)
-    part_b = lax.ppermute(part_a, "pair", SWAP)
-    part_c = lax.ppermute(part_a, "core", SWAP)
-    part_d = lax.ppermute(part_b, "core", SWAP)
+    groups = lax.all_gather(summed, ("far", "high"), axis=0, tiled=False)
+    groups = groups.reshape((FAR, HIGH) + summed.shape)
+    summed = jnp.sum(groups.astype(f32), axis=0).astype(bf16).reshape(-1, width)
+    own = lax.all_gather(summed, ("low", "pair"), axis=0, tiled=True)
+    other = lax.ppermute(own, "core", SWAP)
     (share,) = local(
         second_kernel,
         [((tokens, 2 * width), bf16)],
-        10,
+        8,
         1,
         [pltpu.VMEM((3, width, width), bf16)],
         36 * width * unit,
-    )(place, part_a, part_b, part_c, part_d, q_second, gate_t, up_t, down_memory, out_proj, first_share)
+    )(place, own, other, q_second, gate_t, up_t, down_memory, out_proj, first_share)
     shares = lax.all_to_all(share, ("x", "y"), 0, 0, tiled=True)
     shares = shares.reshape(SIDE * SIDE, -1, 2 * width)
     return jnp.sum(shares.astype(f32), axis=0).astype(bf16)
@@ -168,10 +173,10 @@
 
 def solution(mesh):
     fine = Mesh(
-        mesh.devices.reshape(FAR, MID, PAIR, CORES, SIDE, SIDE),
-        ("far", "mid", "pair", "core", "x", "y"),
+        mesh.devices.reshape(FAR, HIGH, LOW, PAIR, CORES, SIDE, SIDE),
+        ("far", "high", "low", "pair", "core", "x", "y"),
     )
-    seq, head = ("far", "mid", "pair", "core"), ("x", "y")
+    seq, head = ("far", "high", "low", "pair", "core"), ("x", "y")
     in_specs = (
         P(seq, head),
         P(seq, head),

time: 165 us -> 156 us (0.945)
  starting transfers between devices: 31.4 us -> 18.3 us
  blocking collectives: 107 us -> 118 us
  waiting for transfers between devices: 8.47 us -> 1.9 us
    all_gather x1 -> x3, blocking collectives: 44.2 us -> 79 us  [the longest x1 49.3 us: on_device(): groups = lax.all_gather(summed, ('far', 'high'), axis=0, tiled=False)]
    all_to_all x2 -> x1, blocking collectives: 50.6 us -> 25.4 us  [on_device(): lax.all_to_all(pieces, ('low', 'high'), 0, 0, tiled=True)]
    ppermute x4 -> x1, starting transfers between devices: 25.1 us -> 12 us  [on_device(): other = lax.ppermute(own, 'core', SWAP)]
    ppermute x4 -> x1, waiting for transfers between devices: 8.46 us -> 1.89 us  [on_device(): other = lax.ppermute(own, 'core', SWAP)]
  transfers between devices with their start and end apart: 6 -> 3, of which waited for: 3 -> 1; matrix products, arithmetic and copies ran while one was open for 0% -> 0% of each run, Pallas kernels for 0% -> 0%
where the time goes in v4:
time: 156 us; the launch traced here: 155 us
  blocking collectives  118 us (76%)
  starting transfers between devices  18.3 us (12%)
  Pallas kernels  9.54 us (6%)
  local copies, waits for them, and re-layouts  5.13 us (3%)
  other arithmetic  2.11 us (1%)
  waiting for transfers between devices  1.9 us (1%)
    all_gather x1, blocking collectives, on_device(): groups = lax.all_gather(summed, ('far', 'high'), axis=0, tiled=False)  49.3 us
    all_to_all x1, blocking collectives, on_device(): lax.all_to_all(pieces, ('low', 'high'), 0, 0, tiled=True)  25.4 us
    all_gather x1, blocking collectives, on_device(): taken = lax.all_gather(given, 'core', axis=0, tiled=False)  15.7 us
    all_gather x1, blocking collectives, on_device(): own = lax.all_gather(summed, ('low', 'pair'), axis=0, tiled=True)  14 us
    all_to_all x1, blocking collectives, on_device(): shares = lax.all_to_all(share, ('x', 'y'), 0, 0, tiled=True)  13.7 us
    ppermute x1, starting transfers between devices, on_device(): other = lax.ppermute(own, 'core', SWAP)  12 us
    pallas_call x1, Pallas kernels, on_device(): local(second_kernel, [((tokens, 2 * width), bf16)], 8, 1, [pltpu.VMEM((3,...  7.42 us
    unnamed x20, local copies, waits for them, and re-layouts  5.13 us
  transfers between devices with their start and end apart: 3, of which 1 were waited for; matrix products, arithmetic and copies ran while one was open for 0% of the time, Pallas kernels for 0%

profile of v4, /device:TPU:1, one launch (start us, length us, event | category | flops | bytes accessed | tf_op | source)
XLA Modules:
  0.0 155.2 jit_solution(15596608230983582117)
XLA Ops:
  0.0 0.7 copy-done.9
  0.7 1.0 multiply_convert_fusion.scaled_a
  1.7 4.4 %collective-permute-start.1 = (bf16[128,512]{1,0:T(8,128)(2,1)S(1)}, bf16[128,512]{1,0:T(8,128)(2,1)S(1)}, u32[]{:S(2)}, u32[]{:S(2)}) collective-permute-start(bf16[128,512]{1,0:T(8,128)(2,1)S(1)} %multiply_convert_fusion.scaled_a), channel_id=1, source_target_pairs={{0,32},{32,0},{1,33},{33,1},{2,34},{34,2},{3,35},{35,3},{4,36},{36... | collective-permute-start | bytes 393224 | tf_op jit(solution)/shard_map/ppermute | solution.py:133
  6.1 0.0 copy-done.7
  6.1 1.9 %collective-permute-start = (bf16[128,512]{1,0:T(8,128)(2,1)S(1)}, bf16[128,512]{1,0:T(8,128)(2,1)S(1)}, u32[]{:S(2)}, u32[]{:S(2)}) collective-permute-start(bf16[128,512]{1,0:T(8,128)(2,1)S(1)} %copy-done.7), channel_id=1, source_target_pairs={{0,32},{32,0},{1,33},{33,1},{2,34},{34,2},{3,35},{35,3},{4,36},{36... | collective-permute-start | bytes 393224 | tf_op jit(solution)/shard_map/ppermute | solution.py:131
  8.0 0.0 copy-done.6
  8.0 0.0 copy-start
  8.0 1.0 copy-done
  9.1 1.0 copy-done.2
  10.1 1.0 copy-done.3
  11.2 1.0 copy-done.4
  12.2 0.7 shard_map.91
  12.9 0.1 pad_add_fusion.place_ref
  12.9 0.0 collective-permute-done.1.scaled_b
  12.9 0.0 collective-permute-done.keys_b
  13.0 0.3 copy-done.1
  13.2 1.5 shard_map.92
  14.7 15.7 %all-gather = bf16[768,512]{1,0:T(8,128)(2,1)S(1)} all-gather(bf16[384,512]{1,0:T(8,128)(2,1)S(1)} %get-tuple-element.13), channel_id=2, replica_groups=mesh['far'=4,'high'=2,'low'=2,'pair'=2,'core'=2,'x'=4,'y'=4] {'core'}, dimensions={0}, use_global_device_ids=true | all-gather | bytes 1179648 | tf_op jit(solution)/shard_map/all_gather | solution.py:151
  30.4 0.1 fusion
  30.6 25.4 %all_to_all.18 = bf16[4,96,512]{2,1,0:T(8,128)(2,1)S(1)} all-to-all(bf16[4,96,512]{2,1,0:T(8,128)(2,1)S(1)} %bitcast.14), channel_id=1, replica_groups=mesh['far'=4,'high'=2,'low'=2,'pair'=2,'core'=2,'x'=4,'y'=4] {'low','high'}, dimensions={0} | all-to-all | bytes 786432 | tf_op jit(solution)/shard_map/all_to_all | solution.py:154
  56.0 0.1 reduce_sum.36
  56.0 49.3 %all-gather.1 = bf16[768,512]{1,0:T(8,128)(2,1)S(1)} all-gather(bf16[96,512]{1,0:T(8,128)(2,1)S(1)} %reduce_sum.36), channel_id=3, replica_groups=mesh['far'=4,'high'=2,'low'=2,'pair'=2,'core'=2,'x'=4,'y'=4] {'far','high'}, dimensions={0}, use_global_device_ids=true | all-gather | bytes 884736 | tf_op jit(solution)/shard_map/all_gather | solution.py:156
  105.3 0.2 reduce_sum.37
  105.5 0.0 copy-start.5
  105.5 0.0 copy-start.8
  105.5 14.0 %all_gather.19.own_ref = bf16[768,512]{1,0:T(8,128)(2,1)S(1)} all-gather(bf16[192,512]{1,0:T(8,128)(2,1)S(1)} %bitcast.15), channel_id=1, replica_groups=mesh['far'=4,'high'=2,'low'=2,'pair'=2,'core'=2,'x'=4,'y'=4] {'low','pair'}, dimensions={0}, use_global_device_ids=true | all-gather | bytes 983040 | tf_op jit(solution)/shard_map/all_gather | solution.py:159
  119.5 12.0 %collective-permute-start.2 = (bf16[768,512]{1,0:T(8,128)(2,1)S(1)}, bf16[768,512]{1,0:T(8,128)(2,1)S(1)}, u32[]{:S(2)}, u32[]{:S(2)}) collective-permute-start(bf16[768,512]{1,0:T(8,128)(2,1)S(1)} %all_gather.19.own_ref), channel_id=1, source_target_pairs={{0,16},{16,0},{1,17},{17,1},{2,18},{18,2},{3,19},{19,3},{4,20},{20... | collective-permute-start | bytes 2359304 | tf_op jit(solution)/shard_map/ppermute | solution.py:160
  131.5 1.9 %collective-permute-done.2.other_ref = bf16[768,512]{1,0:T(8,128)(2,1)S(1)} collective-permute-done((bf16[768,512]{1,0:T(8,128)(2,1)S(1)}, bf16[768,512]{1,0:T(8,128)(2,1)S(1)}, u32[]{:S(2)}, u32[]{:S(2)}) %collective-permute-start.2) | collective-permute-done | bytes 786464 | tf_op jit(solution)/shard_map/ppermute | solution.py:160
  133.4 0.0 copy-done.5
  133.4 7.4 %shard_map.93 = bf16[128,1024]{1,0:T(8,128)(2,1)S(1)} custom-call(s32[2]{0:T(128)S(1)} %pad_add_fusion.place_ref, bf16[768,512]{1,0:T(8,128)(2,1)S(1)} %all_gather.19.own_ref, bf16[768,512]{1,0:T(8,128)(2,1)S(1)} %collective-permute-done.2.other_ref, bf16[128,512]{1,0:T(8,128)(2,1)S(1)} %copy-done.8, bf16[512,512]{1,0:T(8,128)(2,1)S(1)} %get-tuple-element.10.gate_t_ref, ...), custom_call_target="tpu_custom_call" | custom-call | flops 4831838208 | bytes 3145728 | tf_op jit(solution)/shard_map/pallas_call | solution.py:161
  140.8 13.7 %all_to_all.19 = bf16[16,8,1024]{2,1,0:T(8,128)(2,1)S(1)} all-to-all(bf16[16,8,1024]{2,1,0:T(8,128)(2,1)S(1)} %bitcast.11), channel_id=1, replica_groups=mesh['far'=4,'high'=2,'low'=2,'pair'=2,'core'=2,'x'=4,'y'=4] {'x','y'}, dimensions={0} | all-to-all | bytes 524288 | tf_op jit(solution)/shard_map/all_to_all | solution.py:169
  154.6 0.6 reduce_sum.38
  (8 shorter events, 0.0 us)
Async XLA Ops:
  0.0 0.7 copy-start.9
  0.7 5.4 %copy-start.7 = (bf16[128,512]{1,0:T(8,128)(2,1)S(1)}, bf16[128,512]{1,0:T(8,128)(2,1)}, u32[]{:S(2)}) copy-start(bf16[128,512]{1,0:T(8,128)(2,1)} %keys_a.1) | copy-start | bytes 393220
  0.7 7.4 %copy-start.6 = (bf16[128,512]{1,0:T(8,128)(2,1)S(1)}, bf16[128,512]{1,0:T(8,128)(2,1)}, u32[]{:S(2)}) copy-start(bf16[128,512]{1,0:T(8,128)(2,1)} %q_ref.2) | copy-start | bytes 393220
  1.7 11.3 %collective-permute-start.1 = (bf16[128,512]{1,0:T(8,128)(2,1)S(1)}, bf16[128,512]{1,0:T(8,128)(2,1)S(1)}, u32[]{:S(2)}, u32[]{:S(2)}) collective-permute-start(bf16[128,512]{1,0:T(8,128)(2,1)S(1)} %multiply_convert_fusion.scaled_a), channel_id=1, source_target_pairs={{0,32},{32,0},{1,33},{33,1},{2,34},{34,2},{3,35},{35,3},{4,36},{36... | collective-permute-start | bytes 393224 | tf_op jit(solution)/shard_map/ppermute | solution.py:133
  6.1 6.9 %collective-permute-start = (bf16[128,512]{1,0:T(8,128)(2,1)S(1)}, bf16[128,512]{1,0:T(8,128)(2,1)S(1)}, u32[]{:S(2)}, u32[]{:S(2)}) collective-permute-start(bf16[128,512]{1,0:T(8,128)(2,1)S(1)} %copy-done.7), channel_id=1, source_target_pairs={{0,32},{32,0},{1,33},{33,1},{2,34},{34,2},{3,35},{35,3},{4,36},{36... | collective-permute-start | bytes 393224 | tf_op jit(solution)/shard_map/ppermute | solution.py:131
  8.0 1.0 copy-start
  9.1 1.0 copy-start.2
  10.1 1.0 copy-start.3
  11.2 1.0 copy-start.4
  12.2 1.0 copy-start.1
  105.5 27.9 %copy-start.5 = (bf16[512,512]{1,0:T(8,128)(2,1)S(1)}, bf16[512,512]{1,0:T(8,128)(2,1)}, u32[]{:S(2)}) copy-start(bf16[512,512]{1,0:T(8,128)(2,1)} %proj_ref.3) | copy-start | bytes 1572868
  105.5 27.9 %copy-start.8 = (bf16[128,512]{1,0:T(8,128)(2,1)S(1)}, bf16[128,512]{1,0:T(8,128)(2,1)}, u32[]{:S(2)}) copy-start(bf16[128,512]{1,0:T(8,128)(2,1)} %q_ref.3) | copy-start | bytes 393220
  119.5 13.9 %collective-permute-start.2 = (bf16[768,512]{1,0:T(8,128)(2,1)S(1)}, bf16[768,512]{1,0:T(8,128)(2,1)S(1)}, u32[]{:S(2)}, u32[]{:S(2)}) collective-permute-start(bf16[768,512]{1,0:T(8,128)(2,1)S(1)} %all_gather.19.own_ref), channel_id=1, source_target_pairs={{0,16},{16,0},{1,17},{17,1},{2,18},{18,2},{3,19},{19,3},{4,20},{20... | collective-permute-start | bytes 2359304 | tf_op jit(solution)/shard_map/ppermute | solution.py:160

commit v5 on v4

--- a/solution.py
+++ b/solution.py
@@ -38,17 +38,16 @@
     up_t_ref[...] = up_ref[0].T
 
 
-def descent_kernel(
-    place_ref, keys_a, keys_b, scaled_a, scaled_b, gate_t_ref, up_t_ref, down_ref, kept_ref, given_ref, sums
-):
+def descent_kernel(place_ref, tokens_ref, gate_ref, up_ref, down_ref, kept_ref, given_ref, sums):
     core, pair = place_ref[0], place_ref[1]
+    rows = tokens_ref.shape[0] // (2 * PAIR)
     part = down_ref.shape[1] // PAIR
     half = part // CORES
     units = pl.ds(pl.multiple_of(pair * part, part), part)
-    keys = jnp.concatenate([keys_a[...], keys_b[...]], axis=0)
-    scaled = jnp.concatenate([scaled_a[...], scaled_b[...]], axis=0)
-    gating = dot(gate_t_ref[units, :], keys, (1, 1))
-    lifted = dot(up_t_ref[units, :], keys, (1, 1))
+    keys = jnp.concatenate([tokens_ref[2 * i * rows : (2 * i + 1) * rows] for i in range(PAIR)], axis=0)
+    scaled = jnp.concatenate([tokens_ref[(2 * i + 1) * rows : (2 * i + 2) * rows] for i in range(PAIR)], axis=0)
+    gating = dot(gate_ref[0, :, units].T, keys, (1, 1))
+    lifted = dot(up_ref[0, :, units].T, keys, (1, 1))
     backward = dot(down_ref[0, units, :], scaled, (1, 1))
     s = jax.nn.sigmoid(gating)
     activated = gating * s
@@ -73,20 +72,22 @@
     half = width // PAIR // CORES
     piece = 3 * half // LOW
     step = math.gcd(piece, half)
-    for low in range(LOW):
-        for pair in range(PAIR):
-            for row in range(0, piece, step):
-                m, line = divmod(low * piece + row, half)
-                base = pair * CORES * half + line
-                mine = pl.multiple_of(base + core * half, step)
-                others = pl.multiple_of(base + (1 - core) * half, step)
-                at = (low * PAIR + pair) * piece + row
-                work[m, pl.ds(mine, step), :] = own_ref[at : at + step]
-                work[m, pl.ds(others, step), :] = other_ref[at : at + step]
-    for m in range(3):
-        widened = work[m].astype(f32)
-        magnitude = jnp.sqrt(jnp.sum(widened * widened, keepdims=True)) + 1e-07
-        work[m] = (widened / magnitude).astype(bf16)
+    blocks = []
+    for at in range(0, PAIR * 3 * half, step):
+        source, row = divmod(at, piece)
+        low, pair = divmod(source, PAIR)
+        m, line = divmod(low * piece + row, half)
+        blocks.append((at, m, pair * CORES * half + line))
+    squares = [jnp.zeros((8, width), f32) for m in range(3)]
+    for ref in (own_ref, other_ref):
+        for at, m, base in blocks:
+            widened = ref[at : at + step].astype(f32)
+            squares[m] += jnp.sum((widened * widened).reshape(step // 8, 8, width), axis=0)
+    scales = [1.0 / (jnp.sqrt(jnp.sum(square, keepdims=True)) + 1e-07) for square in squares]
+    for ref, owner in ((own_ref, core), (other_ref, 1 - core)):
+        for at, m, base in blocks:
+            rows = pl.ds(pl.multiple_of(base + owner * half, step), step)
+            work[m, rows, :] = (ref[at : at + step].astype(f32) * scales[m]).astype(bf16)
     for step in range(NS_ITERS):
         for m in range(3):
             current = work[m]
@@ -128,26 +129,17 @@
     tokens, width = keys.shape
     unit = width * width
 
-    keys_next = lax.ppermute(keys, "pair", SWAP)
     scaled = (rates[0][:, None] * values.astype(f32)).astype(bf16)
-    scaled_next = lax.ppermute(scaled, "pair", SWAP)
-    first_share, gate_t, up_t = local(
-        first_kernel,
-        [((tokens, width), bf16), ((width, width), bf16), ((width, width), bf16)],
-        5,
-        0,
-        [],
-        8 * tokens * unit,
-    )(q_first, gate_memory, up_memory, down_memory, out_proj)
+    gathered = lax.all_gather(jnp.concatenate([keys, scaled], axis=0), "pair", axis=0, tiled=True)
     rows = 3 * width // PAIR // CORES
     kept, given = local(
         descent_kernel,
         [((rows, width), f32), ((rows, width), bf16)],
-        7,
+        4,
         1,
         [pltpu.VMEM((3, width // PAIR, width), f32)],
         12 * tokens * unit,
-    )(place, keys, keys_next, scaled, scaled_next, gate_t, up_t, down_memory)
+    )(place, gathered, gate_memory, up_memory, down_memory)
     taken = lax.all_gather(given, "core", axis=0, tiled=False)
     taken = lax.dynamic_index_in_dim(taken, 1 - core, 0, keepdims=False)
     pieces = (kept + taken.astype(f32)).astype(bf16)
@@ -158,6 +150,14 @@
     summed = jnp.sum(groups.astype(f32), axis=0).astype(bf16).reshape(-1, width)
     own = lax.all_gather(summed, ("low", "pair"), axis=0, tiled=True)
     other = lax.ppermute(own, "core", SWAP)
+    first_share, gate_t, up_t = local(
+        first_kernel,
+        [((tokens, width), bf16), ((width, width), bf16), ((width, width), bf16)],
+        5,
+        0,
+        [],
+        8 * tokens * unit,
+    )(q_first, gate_memory, up_memory, down_memory, out_proj)
     (share,) = local(
         second_kernel,
         [((tokens, 2 * width), bf16)],

time: 156 us -> 154 us (0.987)
  blocking collectives: 118 us -> 124 us
  local copies, waits for them, and re-layouts: 5.13 us -> 0.69 us
  starting transfers between devices: 18.3 us -> 14.8 us
    all_gather x0 -> x1, blocking collectives: none -> 7.02 us  [on_device(): lax.all_gather(jnp.concatenate([keys, scaled], axis=0), 'pair', axis=0, t...]
    ppermute x2 -> x0, starting transfers between devices: 6.3 us -> none  [the longest x1 4.38 us: on_device(): scaled_next = lax.ppermute(scaled, 'pair', SWAP)]
    unnamed x20 -> x14, local copies, waits for them, and re-layouts: 5.13 us -> 0.69 us
    ppermute x1, starting transfers between devices: 12 us -> 14.8 us  [on_device(): other = lax.ppermute(own, 'core', SWAP)]
  transfers between devices with their start and end apart: 3 -> 1, of which waited for: 1 -> 1; matrix products, arithmetic and copies ran while one was open for 0% -> 0% of each run, Pallas kernels for 0% -> 0%
where the time goes in v5:
time: 154 us
  blocking collectives  124 us (81%)
  starting transfers between devices  14.8 us (10%)
  Pallas kernels  9.39 us (6%)
  other arithmetic  3.1 us (2%)
    all_gather x1, blocking collectives, on_device(): groups = lax.all_gather(summed, ('far', 'high'), axis=0, tiled=False)  48.2 us
    all_to_all x1, blocking collectives, on_device(): lax.all_to_all(pieces, ('low', 'high'), 0, 0, tiled=True)  25.4 us
    all_gather x1, blocking collectives, on_device(): taken = lax.all_gather(given, 'core', axis=0, tiled=False)  16.3 us
    ppermute x1, starting transfers between devices, on_device(): other = lax.ppermute(own, 'core', SWAP)  14.8 us
    all_to_all x1, blocking collectives, on_device(): shares = lax.all_to_all(share, ('x', 'y'), 0, 0, tiled=True)  14.2 us
    all_gather x1, blocking collectives, on_device(): own = lax.all_gather(summed, ('low', 'pair'), axis=0, tiled=True)  13.2 us
    pallas_call x1, Pallas kernels, on_device(): local(second_kernel, [((tokens, 2 * width), bf16)], 8, 1, [pltpu.VMEM((3,...  7.28 us
    all_gather x1, blocking collectives, on_device(): lax.all_gather(jnp.concatenate([keys, scaled], axis=0), 'pair', axis=0, t...  7.02 us
  transfers between devices with their start and end apart: 1, of which 1 were waited for; matrix products, arithmetic and copies ran while one was open for 0% of the time, Pallas kernels for 0%

profile of v5, /device:TPU:1, one launch (start us, length us, event | category | flops | bytes accessed | tf_op | source)
XLA Modules:
  0.0 153.6 jit_solution(1787371201059496004)
XLA Ops:
  0.0 0.0 copy-start.6
  0.0 0.7 copy-done.6
  0.7 0.0 copy-start.2
  0.7 1.0 multiply_convert_fusion
  1.7 0.0 copy-start.1
  1.7 1.0 pad_maximum_fusion
  2.7 0.0 copy-start
  2.7 7.0 %all_gather.18.tokens_ref = bf16[512,512]{1,0:T(8,128)(2,1)S(1)} all-gather(bf16[256,512]{1,0:T(8,128)(2,1)S(1)} %pad_maximum_fusion), channel_id=1, replica_groups=mesh['far'=4,'high'=2,'low'=2,'pair'=2,'core'=2,'x'=4,'y'=4] {'pair'}, dimensions={0}, use_global_device_ids=true | all-gather | bytes 786432 | tf_op jit(solution)/shard_map/all_gather | solution.py:133
  9.7 0.1 pad_add_fusion.place_ref
  9.8 0.0 copy-done.2
  9.8 0.0 copy-done.1
  9.8 0.0 copy-done
  9.8 1.4 shard_map.91
  11.3 16.3 %all-gather = bf16[768,512]{1,0:T(8,128)(2,1)S(1)} all-gather(bf16[384,512]{1,0:T(8,128)(2,1)S(1)} %get-tuple-element.11), channel_id=2, replica_groups=mesh['far'=4,'high'=2,'low'=2,'pair'=2,'core'=2,'x'=4,'y'=4] {'core'}, dimensions={0}, use_global_device_ids=true | all-gather | bytes 1179648 | tf_op jit(solution)/shard_map/all_gather | solution.py:143
  27.6 0.1 fusion
  27.7 25.4 %all_to_all.18 = bf16[4,96,512]{2,1,0:T(8,128)(2,1)S(1)} all-to-all(bf16[4,96,512]{2,1,0:T(8,128)(2,1)S(1)} %bitcast.14), channel_id=1, replica_groups=mesh['far'=4,'high'=2,'low'=2,'pair'=2,'core'=2,'x'=4,'y'=4] {'low','high'}, dimensions={0} | all-to-all | bytes 786432 | tf_op jit(solution)/shard_map/all_to_all | solution.py:146
  53.1 0.1 reduce_sum.36
  53.2 48.2 %all-gather.1 = bf16[768,512]{1,0:T(8,128)(2,1)S(1)} all-gather(bf16[96,512]{1,0:T(8,128)(2,1)S(1)} %reduce_sum.36), channel_id=3, replica_groups=mesh['far'=4,'high'=2,'low'=2,'pair'=2,'core'=2,'x'=4,'y'=4] {'far','high'}, dimensions={0}, use_global_device_ids=true | all-gather | bytes 884736 | tf_op jit(solution)/shard_map/all_gather | solution.py:148
  101.4 0.2 reduce_sum.37
  101.6 0.0 copy-start.3
  101.6 0.0 copy-start.4
  101.6 13.2 %all_gather.23.own_ref = bf16[768,512]{1,0:T(8,128)(2,1)S(1)} all-gather(bf16[192,512]{1,0:T(8,128)(2,1)S(1)} %bitcast.15), channel_id=1, replica_groups=mesh['far'=4,'high'=2,'low'=2,'pair'=2,'core'=2,'x'=4,'y'=4] {'low','pair'}, dimensions={0}, use_global_device_ids=true | all-gather | bytes 983040 | tf_op jit(solution)/shard_map/all_gather | solution.py:151
  114.8 0.0 copy-start.5
  114.8 14.8 %collective-permute-start = (bf16[768,512]{1,0:T(8,128)(2,1)S(1)}, bf16[768,512]{1,0:T(8,128)(2,1)S(1)}, u32[]{:S(2)}, u32[]{:S(2)}) collective-permute-start(bf16[768,512]{1,0:T(8,128)(2,1)S(1)} %all_gather.23.own_ref), channel_id=1, source_target_pairs={{0,16},{16,0},{1,17},{17,1},{2,18},{18,2},{3,19},{19,3},{4,20},{20... | collective-permute-start | bytes 2359304 | tf_op jit(solution)/shard_map/ppermute | solution.py:152
  129.6 0.0 copy-done.3
  129.6 0.0 copy-done.4
  129.7 0.7 shard_map.92
  130.3 1.2 collective-permute-done.other_ref
  131.5 0.0 copy-done.5
  131.5 7.3 %shard_map.93 = bf16[128,1024]{1,0:T(8,128)(2,1)S(1)} custom-call(s32[2]{0:T(128)S(1)} %pad_add_fusion.place_ref, bf16[768,512]{1,0:T(8,128)(2,1)S(1)} %all_gather.23.own_ref, bf16[768,512]{1,0:T(8,128)(2,1)S(1)} %collective-permute-done.other_ref, bf16[128,512]{1,0:T(8,128)(2,1)S(1)} %copy-done.5, bf16[512,512]{1,0:T(8,128)(2,1)S(1)} %get-tuple-element.12.gate_t_ref, ...), custom_call_target="tpu_custom_call" | custom-call | flops 4831838208 | bytes 3145728 | tf_op jit(solution)/shard_map/pallas_call | solution.py:161
  138.8 14.2 %all_to_all.19 = bf16[16,8,1024]{2,1,0:T(8,128)(2,1)S(1)} all-to-all(bf16[16,8,1024]{2,1,0:T(8,128)(2,1)S(1)} %bitcast.11), channel_id=1, replica_groups=mesh['far'=4,'high'=2,'low'=2,'pair'=2,'core'=2,'x'=4,'y'=4] {'x','y'}, dimensions={0} | all-to-all | bytes 524288 | tf_op jit(solution)/shard_map/all_to_all | solution.py:169
  153.0 0.6 reduce_sum.38
Async XLA Ops:
  0.0 0.7 copy-start.6
  0.7 9.2 %copy-start.2 = (bf16[1,512,512]{2,1,0:T(8,128)(2,1)S(1)}, bf16[1,512,512]{2,1,0:T(8,128)(2,1)}, u32[]{:S(2)}) copy-start(bf16[1,512,512]{2,1,0:T(8,128)(2,1)} %down_ref.5) | copy-start | bytes 1572868
  1.7 8.1 %copy-start.1 = (bf16[1,512,512]{2,1,0:T(8,128)(2,1)S(1)}, bf16[1,512,512]{2,1,0:T(8,128)(2,1)}, u32[]{:S(2)}) copy-start(bf16[1,512,512]{2,1,0:T(8,128)(2,1)} %up_ref.3) | copy-start | bytes 1572868
  2.7 7.1 %copy-start = (bf16[1,512,512]{2,1,0:T(8,128)(2,1)S(1)}, bf16[1,512,512]{2,1,0:T(8,128)(2,1)}, u32[]{:S(2)}) copy-start(bf16[1,512,512]{2,1,0:T(8,128)(2,1)} %gate_ref.3) | copy-start | bytes 1572868
  101.6 28.0 %copy-start.3 = (bf16[512,512]{1,0:T(8,128)(2,1)S(1)}, bf16[512,512]{1,0:T(8,128)(2,1)}, u32[]{:S(2)}) copy-start(bf16[512,512]{1,0:T(8,128)(2,1)} %proj_ref.3) | copy-start | bytes 1572868
  101.6 28.0 %copy-start.4 = (bf16[128,512]{1,0:T(8,128)(2,1)S(1)}, bf16[128,512]{1,0:T(8,128)(2,1)}, u32[]{:S(2)}) copy-start(bf16[128,512]{1,0:T(8,128)(2,1)} %q_ref.2) | copy-start | bytes 393220
  114.8 16.7 %copy-start.5 = (bf16[128,512]{1,0:T(8,128)(2,1)S(1)}, bf16[128,512]{1,0:T(8,128)(2,1)}, u32[]{:S(2)}) copy-start(bf16[128,512]{1,0:T(8,128)(2,1)} %q_ref.3) | copy-start | bytes 393220
  114.8 16.7 %collective-permute-start = (bf16[768,512]{1,0:T(8,128)(2,1)S(1)}, bf16[768,512]{1,0:T(8,128)(2,1)S(1)}, u32[]{:S(2)}, u32[]{:S(2)}) collective-permute-start(bf16[768,512]{1,0:T(8,128)(2,1)S(1)} %all_gather.23.own_ref), channel_id=1, source_target_pairs={{0,16},{16,0},{1,17},{17,1},{2,18},{18,2},{3,19},{19,3},{4,20},{20... | collective-permute-start | bytes 2359304 | tf_op jit(solution)/shard_map/ppermute | solution.py:152

commit v6 on v5

--- a/solution.py
+++ b/solution.py
@@ -9,7 +9,7 @@
 from jax.sharding import PartitionSpec as P
 
 NS_ITERS = 2
-FAR, HIGH, LOW, PAIR, CORES, SIDE = 4, 2, 2, 2, 2, 4
+TOP, FAR, HIGH, LOW, PAIR, CORES, SIDE = 2, 2, 2, 2, 2, 2, 4
 VMEM_BYTES = 48 * 1024 * 1024
 
 first_coeff = 3.4445
@@ -144,10 +144,18 @@
     taken = lax.dynamic_index_in_dim(taken, 1 - core, 0, keepdims=False)
     pieces = (kept + taken.astype(f32)).astype(bf16)
     pieces = lax.all_to_all(pieces, ("low", "high"), 0, 0, tiled=True).reshape(HIGH * LOW, -1, width)
-    summed = jnp.sum(pieces.astype(f32), axis=0).astype(bf16)
-    groups = lax.all_gather(summed, ("far", "high"), axis=0, tiled=False)
-    groups = groups.reshape((FAR, HIGH) + summed.shape)
-    summed = jnp.sum(groups.astype(f32), axis=0).astype(bf16).reshape(-1, width)
+    far = lax.axis_index("far")
+    halves = jnp.sum(pieces.astype(f32), axis=0).reshape(FAR, -1, width)
+    taken = lax.all_gather(
+        lax.dynamic_index_in_dim(halves, 1 - far, 0, keepdims=False).astype(bf16), "far", axis=0, tiled=False
+    )
+    taken = lax.dynamic_index_in_dim(taken, 1 - far, 0, keepdims=False)
+    summed = (lax.dynamic_index_in_dim(halves, far, 0, keepdims=False) + taken.astype(f32)).astype(bf16)
+    groups = lax.all_gather(summed, ("top", "far", "high", "core"), axis=0, tiled=False)
+    groups = groups.reshape((TOP, FAR, HIGH, CORES) + summed.shape)
+    groups = lax.dynamic_index_in_dim(groups, core, 3, keepdims=False)
+    summed = jnp.sum(groups.astype(f32), axis=0).astype(bf16)
+    summed = summed.transpose(1, 0, 2, 3).reshape(-1, width)
     own = lax.all_gather(summed, ("low", "pair"), axis=0, tiled=True)
     other = lax.ppermute(own, "core", SWAP)
     first_share, gate_t, up_t = local(
@@ -173,10 +181,10 @@
 
 def solution(mesh):
     fine = Mesh(
-        mesh.devices.reshape(FAR, HIGH, LOW, PAIR, CORES, SIDE, SIDE),
-        ("far", "high", "low", "pair", "core", "x", "y"),
-    )
-    seq, head = ("far", "high", "low", "pair", "core"), ("x", "y")
+        mesh.devices.reshape(TOP, FAR, HIGH, LOW, PAIR, CORES, SIDE, SIDE),
+        ("top", "far", "high", "low", "pair", "core", "x", "y"),
+    )
+    seq, head = ("top", "far", "high", "low", "pair", "core"), ("x", "y")
     in_specs = (
         P(seq, head),
         P(seq, head),

time: 154 us -> 153 us (level)
  waiting for transfers between devices: 1.2 us -> 24.2 us
  blocking collectives: 124 us -> 108 us
  starting transfers between devices: 14.8 us -> 6.72 us
    all_to_all x1 -> x0, blocking collectives: 25.4 us -> none  [on_device(): lax.all_to_all(pieces, ('low', 'high'), 0, 0, tiled=True)]
    all_to_all x0 -> x1, waiting for transfers between devices: none -> 23 us  [on_device(): lax.all_to_all(pieces, ('low', 'high'), 0, 0, tiled=True)]
    ppermute x1, starting transfers between devices: 14.8 us -> 3.26 us  [on_device(): other = lax.ppermute(own, 'core', SWAP)]
    all_gather x1, blocking collectives: 13.2 us -> 18.8 us  [on_device(): own = lax.all_gather(summed, ('low', 'pair'), axis=0, tiled=True)]
    all_to_all x0 -> x1, starting transfers between devices: none -> 3.46 us  [on_device(): lax.all_to_all(pieces, ('low', 'high'), 0, 0, tiled=True)]
    all_to_all x1, blocking collectives: 14.2 us -> 16.5 us  [on_device(): shares = lax.all_to_all(share, ('x', 'y'), 0, 0, tiled=True)]
    all_gather x1 -> x2, blocking collectives: 48.2 us -> 49 us  [the longest x1 30.2 us: on_device(): lax.all_gather(summed, ('top', 'far', 'high', 'core'), axis=0, tiled=False)]
  transfers between devices with their start and end apart: 1 -> 2, of which waited for: 1 -> 2; matrix products, arithmetic and copies ran while one was open for 0% -> 0% of each run, Pallas kernels for 0% -> 0%
where the time goes in v6:
time: 153 us; the launch traced here: 152 us
  blocking collectives  108 us (71%)
  waiting for transfers between devices  24.2 us (16%)
  Pallas kernels  9.39 us (6%)
  starting transfers between devices  6.72 us (4%)
  other arithmetic  3.75 us (2%)
    all_gather x1, blocking collectives, on_device(): lax.all_gather(summed, ('top', 'far', 'high', 'core'), axis=0, tiled=False)  30.2 us
    all_to_all x1, waiting for transfers between devices, on_device(): lax.all_to_all(pieces, ('low', 'high'), 0, 0, tiled=True)  23 us
    all_gather x1, blocking collectives, on_device(): own = lax.all_gather(summed, ('low', 'pair'), axis=0, tiled=True)  18.8 us
    all_gather x1, blocking collectives, on_device(): lax.all_gather(lax.dynamic_index_in_dim(halves, 1 - far, 0, keepdims=Fals...  18.8 us
    all_to_all x1, blocking collectives, on_device(): shares = lax.all_to_all(share, ('x', 'y'), 0, 0, tiled=True)  16.5 us
    all_gather x1, blocking collectives, on_device(): taken = lax.all_gather(given, 'core', axis=0, tiled=False)  16.3 us
    pallas_call x1, Pallas kernels, on_device(): local(second_kernel, [((tokens, 2 * width), bf16)], 8, 1, [pltpu.VMEM((3,...  7.28 us
    all_gather x1, blocking collectives, on_device(): lax.all_gather(jnp.concatenate([keys, scaled], axis=0), 'pair', axis=0, t...  7.02 us
  transfers between devices with their start and end apart: 2, of which 2 were waited for; matrix products, arithmetic and copies ran while one was open for 0% of the time, Pallas kernels for 0%

profile of v6, /device:TPU:1, one launch (start us, length us, event | category | flops | bytes accessed | tf_op | source)
XLA Modules:
  0.0 152.5 jit_solution(13937907993748658517)
XLA Ops:
  0.0 0.0 copy-start.6
  0.0 0.7 copy-done.6
  0.7 1.0 multiply_convert_fusion
  1.7 0.0 copy-start.1
  1.7 1.0 pad_maximum_fusion
  2.7 0.0 copy-start
  2.7 7.0 %all_gather.20.tokens_ref = bf16[512,512]{1,0:T(8,128)(2,1)S(1)} all-gather(bf16[256,512]{1,0:T(8,128)(2,1)S(1)} %pad_maximum_fusion), channel_id=1, replica_groups=mesh['top'=2,'far'=2,'high'=2,'low'=2,'pair'=2,'core'=2,'x'=4,'y'=4] {'p..., dimensions={0}, use_global_device_ids=true | all-gather | bytes 786432 | tf_op jit(solution)/shard_map/all_gather | solution.py:133
  9.7 0.1 pad_add_fusion.place_ref
  9.8 0.0 copy-done.2
  9.8 0.0 copy-done.1
  9.8 0.0 copy-done
  9.8 1.4 shard_map.91
  11.3 16.3 %all-gather = bf16[768,512]{1,0:T(8,128)(2,1)S(1)} all-gather(bf16[384,512]{1,0:T(8,128)(2,1)S(1)} %get-tuple-element.11), channel_id=2, replica_groups=mesh['top'=2,'far'=2,'high'=2,'low'=2,'pair'=2,'core'=2,'x'=4,'y'=4] {'c..., dimensions={0}, use_global_device_ids=true | all-gather | bytes 1179648 | tf_op jit(solution)/shard_map/all_gather | solution.py:143
  27.6 0.9 fusion
  28.5 3.5 %all-to-all-start = ((bf16[4,96,512]{2,1,0:T(8,128)(2,1)}), bf16[4,96,512]{2,1,0:T(8,128)(2,1)S(1)}, u32[]{:S(2)}, u32[]{:S(2)}) async-start(bf16[4,96,512]{2,1,0:T(8,128)(2,1)} %bitcast.5), calls=%async_computation | async-start | bytes 786432 | tf_op jit(solution)/shard_map/all_to_all | solution.py:146
  31.9 23.0 %all-to-all-done = bf16[4,96,512]{2,1,0:T(8,128)(2,1)S(1)} async-done(((bf16[4,96,512]{2,1,0:T(8,128)(2,1)}), bf16[4,96,512]{2,1,0:T(8,128)(2,1)S(1)}, u32[]{:S(2)}, u32[]{:S(2)}) %all-to-all-start) | async-done | bytes 393248 | tf_op jit(solution)/shard_map/all_to_all | solution.py:146
  54.9 0.1 convert_reduce_fusion
  55.0 18.8 %all_gather.23 = bf16[2,48,512]{2,1,0:T(8,128)(2,1)S(1)} all-gather(bf16[1,48,512]{2,1,0:T(8,128)(2,1)S(1)} %dynamic-slice_convert_fusion), channel_id=1, replica_groups=mesh['top'=2,'far'=2,'high'=2,'low'=2,'pair'=2,'core'=2,'x'=4,'y'=4] {'f..., dimensions={0}, use_global_device_ids=true | all-gather | bytes 147456 | tf_op jit(solution)/shard_map/all_gather | solution.py:149
  73.8 30.2 %all_gather.24 = bf16[16,48,512]{2,1,0:T(8,128)(2,1)S(1)} all-gather(bf16[1,48,512]{2,1,0:T(8,128)(2,1)S(1)} %add_convert_fusion), channel_id=1, replica_groups=mesh['top'=2,'far'=2,'high'=2,'low'=2,'pair'=2,'core'=2,'x'=4,'y'=4] {'t..., dimensions={0}, use_global_device_ids=true | all-gather | bytes 835584 | tf_op jit(solution)/shard_map/all_gather | solution.py:154
  104.0 0.1 dynamic-slice_reduce_fusion
  104.1 0.0 copy-start.3
  104.1 0.0 copy-start.4
  104.1 18.8 %all_gather.25.own_ref = bf16[768,512]{1,0:T(8,128)(2,1)S(1)} all-gather(bf16[192,512]{1,0:T(8,128)(2,1)S(1)} %bitcast.17), channel_id=1, replica_groups=mesh['top'=2,'far'=2,'high'=2,'low'=2,'pair'=2,'core'=2,'x'=4,'y'=4] {'l..., dimensions={0}, use_global_device_ids=true | all-gather | bytes 983040 | tf_op jit(solution)/shard_map/all_gather | solution.py:159
  122.9 3.3 %collective-permute-start = (bf16[768,512]{1,0:T(8,128)(2,1)S(1)}, bf16[768,512]{1,0:T(8,128)(2,1)S(1)}, u32[]{:S(2)}, u32[]{:S(2)}) collective-permute-start(bf16[768,512]{1,0:T(8,128)(2,1)S(1)} %all_gather.25.own_ref), channel_id=1, source_target_pairs={{0,16},{16,0},{1,17},{17,1},{2,18},{18,2},{3,19},{19,3},{4,20},{20... | collective-permute-start | bytes 2359304 | tf_op jit(solution)/shard_map/ppermute | solution.py:160
  126.2 0.0 copy-done.3
  126.2 0.0 copy-done.4
  126.2 0.7 shard_map.92
  126.9 1.2 collective-permute-done.other_ref
  128.1 0.0 copy-done.5
  128.1 7.3 %shard_map.93 = bf16[128,1024]{1,0:T(8,128)(2,1)S(1)} custom-call(s32[2]{0:T(128)S(1)} %pad_add_fusion.place_ref, bf16[768,512]{1,0:T(8,128)(2,1)S(1)} %all_gather.25.own_ref, bf16[768,512]{1,0:T(8,128)(2,1)S(1)} %collective-permute-done.other_ref, bf16[128,512]{1,0:T(8,128)(2,1)S(1)} %copy-done.5, bf16[512,512]{1,0:T(8,128)(2,1)S(1)} %get-tuple-element.12.gate_t_ref, ...), custom_call_target="tpu_custom_call" | custom-call | flops 4831838208 | bytes 3145728 | tf_op jit(solution)/shard_map/pallas_call | solution.py:169
  135.4 16.5 %all_to_all.18 = bf16[16,8,1024]{2,1,0:T(8,128)(2,1)S(1)} all-to-all(bf16[16,8,1024]{2,1,0:T(8,128)(2,1)S(1)} %bitcast.13), channel_id=1, replica_groups=mesh['top'=2,'far'=2,'high'=2,'low'=2,'pair'=2,'core'=2,'x'=4,'y'=4] {'x..., dimensions={0} | all-to-all | bytes 524288 | tf_op jit(solution)/shard_map/all_to_all | solution.py:177
  151.8 0.6 reduce_sum.35
  (5 shorter events, 0.0 us)
Async XLA Ops:
  0.0 0.7 copy-start.6
  0.7 9.2 %copy-start.2 = (bf16[1,512,512]{2,1,0:T(8,128)(2,1)S(1)}, bf16[1,512,512]{2,1,0:T(8,128)(2,1)}, u32[]{:S(2)}) copy-start(bf16[1,512,512]{2,1,0:T(8,128)(2,1)} %down_ref.5) | copy-start | bytes 1572868
  1.7 8.1 %copy-start.1 = (bf16[1,512,512]{2,1,0:T(8,128)(2,1)S(1)}, bf16[1,512,512]{2,1,0:T(8,128)(2,1)}, u32[]{:S(2)}) copy-start(bf16[1,512,512]{2,1,0:T(8,128)(2,1)} %up_ref.3) | copy-start | bytes 1572868
  2.7 7.1 %copy-start = (bf16[1,512,512]{2,1,0:T(8,128)(2,1)S(1)}, bf16[1,512,512]{2,1,0:T(8,128)(2,1)}, u32[]{:S(2)}) copy-start(bf16[1,512,512]{2,1,0:T(8,128)(2,1)} %gate_ref.3) | copy-start | bytes 1572868
  28.5 26.4 %all-to-all-start = ((bf16[4,96,512]{2,1,0:T(8,128)(2,1)}), bf16[4,96,512]{2,1,0:T(8,128)(2,1)S(1)}, u32[]{:S(2)}, u32[]{:S(2)}) async-start(bf16[4,96,512]{2,1,0:T(8,128)(2,1)} %bitcast.5), calls=%async_computation | async-start | bytes 786432 | tf_op jit(solution)/shard_map/all_to_all | solution.py:146
  104.1 22.1 %copy-start.3 = (bf16[512,512]{1,0:T(8,128)(2,1)S(1)}, bf16[512,512]{1,0:T(8,128)(2,1)}, u32[]{:S(2)}) copy-start(bf16[512,512]{1,0:T(8,128)(2,1)} %proj_ref.3) | copy-start | bytes 1572868
  104.1 22.1 %copy-start.4 = (bf16[128,512]{1,0:T(8,128)(2,1)S(1)}, bf16[128,512]{1,0:T(8,128)(2,1)}, u32[]{:S(2)}) copy-start(bf16[128,512]{1,0:T(8,128)(2,1)} %q_ref.2) | copy-start | bytes 393220
  122.9 5.2 %copy-start.5 = (bf16[128,512]{1,0:T(8,128)(2,1)S(1)}, bf16[128,512]{1,0:T(8,128)(2,1)}, u32[]{:S(2)}) copy-start(bf16[128,512]{1,0:T(8,128)(2,1)} %q_ref.3) | copy-start | bytes 393220
  122.9 5.2 %collective-permute-start = (bf16[768,512]{1,0:T(8,128)(2,1)S(1)}, bf16[768,512]{1,0:T(8,128)(2,1)S(1)}, u32[]{:S(2)}, u32[]{:S(2)}) collective-permute-start(bf16[768,512]{1,0:T(8,128)(2,1)S(1)} %all_gather.25.own_ref), channel_id=1, source_target_pairs={{0,16},{16,0},{1,17},{17,1},{2,18},{18,2},{3,19},{19,3},{4,20},{20... | collective-permute-start | bytes 2359304 | tf_op jit(solution)/shard_map/ppermute | solution.py:160

commit v7 on v6

--- a/solution.py
+++ b/solution.py
@@ -71,12 +71,14 @@
     width = q_ref.shape[1]
     half = width // PAIR // CORES
     piece = 3 * half // LOW
-    step = math.gcd(piece, half)
+    share = piece // FAR // HIGH
+    step = math.gcd(share, half)
     blocks = []
     for at in range(0, PAIR * 3 * half, step):
         source, row = divmod(at, piece)
         low, pair = divmod(source, PAIR)
-        m, line = divmod(low * piece + row, half)
+        far, high = divmod(row // share, HIGH)
+        m, line = divmod(((low * HIGH + high) * FAR + far) * share + row % share, half)
         blocks.append((at, m, pair * CORES * half + line))
     squares = [jnp.zeros((8, width), f32) for m in range(3)]
     for ref in (own_ref, other_ref):
@@ -141,21 +143,21 @@
         12 * tokens * unit,
     )(place, gathered, gate_memory, up_memory, down_memory)
     taken = lax.all_gather(given, "core", axis=0, tiled=False)
-    taken = lax.dynamic_index_in_dim(taken, 1 - core, 0, keepdims=False)
+    taken = jnp.where(core == 0, taken[1], taken[0])
     pieces = (kept + taken.astype(f32)).astype(bf16)
     pieces = lax.all_to_all(pieces, ("low", "high"), 0, 0, tiled=True).reshape(HIGH * LOW, -1, width)
     far = lax.axis_index("far")
     halves = jnp.sum(pieces.astype(f32), axis=0).reshape(FAR, -1, width)
     taken = lax.all_gather(
-        lax.dynamic_index_in_dim(halves, 1 - far, 0, keepdims=False).astype(bf16), "far", axis=0, tiled=False
-    )
-    taken = lax.dynamic_index_in_dim(taken, 1 - far, 0, keepdims=False)
-    summed = (lax.dynamic_index_in_dim(halves, far, 0, keepdims=False) + taken.astype(f32)).astype(bf16)
+        jnp.where(far == 0, halves[1], halves[0]).astype(bf16), "far", axis=0, tiled=False
+    )
+    taken = jnp.where(far == 0, taken[1], taken[0])
+    summed = (jnp.where(far == 0, halves[0], halves[1]) + taken.astype(f32)).astype(bf16)
     groups = lax.all_gather(summed, ("top", "far", "high", "core"), axis=0, tiled=False)
     groups = groups.reshape((TOP, FAR, HIGH, CORES) + summed.shape)
-    groups = lax.dynamic_index_in_dim(groups, core, 3, keepdims=False)
+    groups = jnp.where(core == 0, groups[:, :, :, 0], groups[:, :, :, 1])
     summed = jnp.sum(groups.astype(f32), axis=0).astype(bf16)
-    summed = summed.transpose(1, 0, 2, 3).reshape(-1, width)
+    summed = summed.reshape(-1, width)
     own = lax.all_gather(summed, ("low", "pair"), axis=0, tiled=True)
     other = lax.ppermute(own, "core", SWAP)
     first_share, gate_t, up_t = local(

time: 153 us -> 153 us (level)
  no operation moved by 1% of the time
where the time goes in v7:
time: 153 us
  blocking collectives  108 us (71%)
  waiting for transfers between devices  24.2 us (16%)
  Pallas kernels  9.51 us (6%)
  starting transfers between devices  6.72 us (4%)
  other arithmetic  3.88 us (3%)
    all_gather x1, blocking collectives, on_device(): lax.all_gather(summed, ('top', 'far', 'high', 'core'), axis=0, tiled=False)  31.3 us
    all_to_all x1, waiting for transfers between devices, on_device(): lax.all_to_all(pieces, ('low', 'high'), 0, 0, tiled=True)  23 us
    all_gather x1, blocking collectives, on_device(): lax.all_gather(jnp.where(far == 0, halves[1], halves[0]).astype(bf16), 'f...  18.8 us
    all_gather x1, blocking collectives, on_device(): own = lax.all_gather(summed, ('low', 'pair'), axis=0, tiled=True)  17.7 us
    all_to_all x1, blocking collectives, on_device(): shares = lax.all_to_all(share, ('x', 'y'), 0, 0, tiled=True)  16.5 us
    all_gather x1, blocking collectives, on_device(): taken = lax.all_gather(given, 'core', axis=0, tiled=False)  16.3 us
    pallas_call x1, Pallas kernels, on_device(): local(second_kernel, [((tokens, 2 * width), bf16)], 8, 1, [pltpu.VMEM((3,...  7.41 us
    all_gather x1, blocking collectives, on_device(): lax.all_gather(jnp.concatenate([keys, scaled], axis=0), 'pair', axis=0, t...  7.02 us
  transfers between devices with their start and end apart: 2, of which 2 were waited for; matrix products, arithmetic and copies ran while one was open for 0% of the time, Pallas kernels for 0%

profile of v7, /device:TPU:1, one launch (start us, length us, event | category | flops | bytes accessed | tf_op | source)
XLA Modules:
  0.0 152.7 jit_solution(10503474504202889204)
XLA Ops:
  0.0 0.0 copy-start.6
  0.0 0.7 copy-done.6
  0.7 1.0 multiply_convert_fusion
  1.7 0.0 copy-start.1
  1.7 1.0 pad_maximum_fusion
  2.7 0.0 copy-start
  2.7 7.0 %all_gather.24.tokens_ref = bf16[512,512]{1,0:T(8,128)(2,1)S(1)} all-gather(bf16[256,512]{1,0:T(8,128)(2,1)S(1)} %pad_maximum_fusion), channel_id=1, replica_groups=mesh['top'=2,'far'=2,'high'=2,'low'=2,'pair'=2,'core'=2,'x'=4,'y'=4] {'p..., dimensions={0}, use_global_device_ids=true | all-gather | bytes 786432 | tf_op jit(solution)/shard_map/all_gather | solution.py:135
  9.7 0.1 pad_add_fusion.place_ref
  9.8 0.0 copy-done.2
  9.8 0.0 copy-done.1
  9.8 0.0 copy-done
  9.8 1.4 shard_map.91
  11.3 16.3 %all-gather = bf16[768,512]{1,0:T(8,128)(2,1)S(1)} all-gather(bf16[384,512]{1,0:T(8,128)(2,1)S(1)} %get-tuple-element.11), channel_id=2, replica_groups=mesh['top'=2,'far'=2,'high'=2,'low'=2,'pair'=2,'core'=2,'x'=4,'y'=4] {'c..., dimensions={0}, use_global_device_ids=true | all-gather | bytes 1179648 | tf_op jit(solution)/shard_map/all_gather | solution.py:145
  27.6 0.9 fusion
  28.5 3.5 %all-to-all-start = ((bf16[4,96,512]{2,1,0:T(8,128)(2,1)}), bf16[4,96,512]{2,1,0:T(8,128)(2,1)S(1)}, u32[]{:S(2)}, u32[]{:S(2)}) async-start(bf16[4,96,512]{2,1,0:T(8,128)(2,1)} %bitcast.3), calls=%async_computation | async-start | bytes 786432 | tf_op jit(solution)/shard_map/all_to_all | solution.py:148
  32.0 23.0 %all-to-all-done = bf16[4,96,512]{2,1,0:T(8,128)(2,1)S(1)} async-done(((bf16[4,96,512]{2,1,0:T(8,128)(2,1)}), bf16[4,96,512]{2,1,0:T(8,128)(2,1)S(1)}, u32[]{:S(2)}, u32[]{:S(2)}) %all-to-all-start) | async-done | bytes 393248 | tf_op jit(solution)/shard_map/all_to_all | solution.py:148
  54.9 0.1 convert_reduce_fusion
  55.0 18.8 %all-gather.1 = bf16[96,512]{1,0:T(8,128)(2,1)S(1)} all-gather(bf16[48,512]{1,0:T(8,128)(2,1)S(1)} %select_convert_fusion), channel_id=3, replica_groups=mesh['top'=2,'far'=2,'high'=2,'low'=2,'pair'=2,'core'=2,'x'=4,'y'=4] {'f..., dimensions={0}, use_global_device_ids=true | all-gather | bytes 147456 | tf_op jit(solution)/shard_map/all_gather | solution.py:151
  73.8 31.3 %all-gather.2 = bf16[768,512]{1,0:T(8,128)(2,1)S(1)} all-gather(bf16[48,512]{1,0:T(8,128)(2,1)S(1)} %fusion.2), channel_id=4, replica_groups=mesh['top'=2,'far'=2,'high'=2,'low'=2,'pair'=2,'core'=2,'x'=4,'y'=4] {'t..., dimensions={0}, use_global_device_ids=true | all-gather | bytes 835584 | tf_op jit(solution)/shard_map/all_gather | solution.py:156
  105.2 0.1 fusion.1
  105.3 0.0 copy-start.3
  105.3 0.0 copy-start.4
  105.3 17.7 %all_gather.31.own_ref = bf16[768,512]{1,0:T(8,128)(2,1)S(1)} all-gather(bf16[192,512]{1,0:T(8,128)(2,1)S(1)} %bitcast.9), channel_id=1, replica_groups=mesh['top'=2,'far'=2,'high'=2,'low'=2,'pair'=2,'core'=2,'x'=4,'y'=4] {'l..., dimensions={0}, use_global_device_ids=true | all-gather | bytes 983040 | tf_op jit(solution)/shard_map/all_gather | solution.py:161
  123.0 3.3 %collective-permute-start = (bf16[768,512]{1,0:T(8,128)(2,1)S(1)}, bf16[768,512]{1,0:T(8,128)(2,1)S(1)}, u32[]{:S(2)}, u32[]{:S(2)}) collective-permute-start(bf16[768,512]{1,0:T(8,128)(2,1)S(1)} %all_gather.31.own_ref), channel_id=1, source_target_pairs={{0,16},{16,0},{1,17},{17,1},{2,18},{18,2},{3,19},{19,3},{4,20},{20... | collective-permute-start | bytes 2359304 | tf_op jit(solution)/shard_map/ppermute | solution.py:162
  126.3 0.0 copy-done.3
  126.3 0.0 copy-done.4
  126.3 0.7 shard_map.92
  127.0 1.2 collective-permute-done.other_ref
  128.2 0.0 copy-done.5
  128.2 7.4 %shard_map.93 = bf16[128,1024]{1,0:T(8,128)(2,1)S(1)} custom-call(s32[2]{0:T(128)S(1)} %pad_add_fusion.place_ref, bf16[768,512]{1,0:T(8,128)(2,1)S(1)} %all_gather.31.own_ref, bf16[768,512]{1,0:T(8,128)(2,1)S(1)} %collective-permute-done.other_ref, bf16[128,512]{1,0:T(8,128)(2,1)S(1)} %copy-done.5, bf16[512,512]{1,0:T(8,128)(2,1)S(1)} %get-tuple-element.12.gate_t_ref, ...), custom_call_target="tpu_custom_call" | custom-call | flops 4831838208 | bytes 3145728 | tf_op jit(solution)/shard_map/pallas_call | solution.py:171
  135.6 16.5 %all_to_all.18 = bf16[16,8,1024]{2,1,0:T(8,128)(2,1)S(1)} all-to-all(bf16[16,8,1024]{2,1,0:T(8,128)(2,1)S(1)} %bitcast.7), channel_id=1, replica_groups=mesh['top'=2,'far'=2,'high'=2,'low'=2,'pair'=2,'core'=2,'x'=4,'y'=4] {'x..., dimensions={0} | all-to-all | bytes 524288 | tf_op jit(solution)/shard_map/all_to_all | solution.py:179
  152.0 0.6 reduce_sum.35
  (4 shorter events, 0.0 us)
Async XLA Ops:
  0.0 0.7 copy-start.6
  0.7 9.2 %copy-start.2 = (bf16[1,512,512]{2,1,0:T(8,128)(2,1)S(1)}, bf16[1,512,512]{2,1,0:T(8,128)(2,1)}, u32[]{:S(2)}) copy-start(bf16[1,512,512]{2,1,0:T(8,128)(2,1)} %down_ref.5) | copy-start | bytes 1572868
  1.7 8.1 %copy-start.1 = (bf16[1,512,512]{2,1,0:T(8,128)(2,1)S(1)}, bf16[1,512,512]{2,1,0:T(8,128)(2,1)}, u32[]{:S(2)}) copy-start(bf16[1,512,512]{2,1,0:T(8,128)(2,1)} %up_ref.3) | copy-start | bytes 1572868
  2.7 7.1 %copy-start = (bf16[1,512,512]{2,1,0:T(8,128)(2,1)S(1)}, bf16[1,512,512]{2,1,0:T(8,128)(2,1)}, u32[]{:S(2)}) copy-start(bf16[1,512,512]{2,1,0:T(8,128)(2,1)} %gate_ref.3) | copy-start | bytes 1572868
  28.5 26.5 %all-to-all-start = ((bf16[4,96,512]{2,1,0:T(8,128)(2,1)}), bf16[4,96,512]{2,1,0:T(8,128)(2,1)S(1)}, u32[]{:S(2)}, u32[]{:S(2)}) async-start(bf16[4,96,512]{2,1,0:T(8,128)(2,1)} %bitcast.3), calls=%async_computation | async-start | bytes 786432 | tf_op jit(solution)/shard_map/all_to_all | solution.py:148
  105.3 21.0 %copy-start.3 = (bf16[512,512]{1,0:T(8,128)(2,1)S(1)}, bf16[512,512]{1,0:T(8,128)(2,1)}, u32[]{:S(2)}) copy-start(bf16[512,512]{1,0:T(8,128)(2,1)} %proj_ref.3) | copy-start | bytes 1572868
  105.3 21.0 %copy-start.4 = (bf16[128,512]{1,0:T(8,128)(2,1)S(1)}, bf16[128,512]{1,0:T(8,128)(2,1)}, u32[]{:S(2)}) copy-start(bf16[128,512]{1,0:T(8,128)(2,1)} %q_ref.2) | copy-start | bytes 393220
  123.0 5.2 %copy-start.5 = (bf16[128,512]{1,0:T(8,128)(2,1)S(1)}, bf16[128,512]{1,0:T(8,128)(2,1)}, u32[]{:S(2)}) copy-start(bf16[128,512]{1,0:T(8,128)(2,1)} %q_ref.3) | copy-start | bytes 393220
  123.0 5.2 %collective-permute-start = (bf16[768,512]{1,0:T(8,128)(2,1)S(1)}, bf16[768,512]{1,0:T(8,128)(2,1)S(1)}, u32[]{:S(2)}, u32[]{:S(2)}) collective-permute-start(bf16[768,512]{1,0:T(8,128)(2,1)S(1)} %all_gather.31.own_ref), channel_id=1, source_target_pairs={{0,16},{16,0},{1,17},{17,1},{2,18},{18,2},{3,19},{19,3},{4,20},{20... | collective-permute-start | bytes 2359304 | tf_op jit(solution)/shard_map/ppermute | solution.py:162
